TPU v7x, 32 devices: a whole 2x2x4 slice. The times are simulated.
32 devices in a mesh: curve: 16 (over z, y, x), sub: 2 (over core).
Axes of the slice: x: 2, y: 2, z: 4, core: 2. Of those that a mesh axis runs over, the one named last changes fastest.
Arguments:
- pressure: float32 [128, 4096], P(('curve', 'sub')), may hold values from -6 to 6
- source_term: float32 [128, 4096], P(('curve', 'sub')), may hold values from -7 to 7
- coefficient: float32 [128, 4096], P(('curve', 'sub')), may hold values from 0.05 to 2
- new_slot: int32 [128], P(('curve', 'sub')), may hold values from 0 to 7, as said below
- face_links: int32 [128, 6], P(('curve', 'sub')), may hold values from -1 to 127, as said below
Outputs:
- corrected: float32 [128, 4096], P(('curve', 'sub'))
Inputs may be any that keep to these rules, and one draw needn't show every extreme that they name: `new_slot`: every block stays within its Z-order range of 8 blocks; within a range the slots form a permutation, each device receives exactly 4 blocks, and one device hands at most 2 blocks to one device, a bound reached by every device. `face_links`: A neighbour of block b lies in range b // 8 - 1, b // 8 or b // 8 + 1.
All inputs are finite; a program needn't handle non-finite values.
Results may differ from a plain program's by a relative error of at most 0.0001.
Values sent between devices are 32-bit elements; how exact they have to be, the bound alone decides.
A program may use at most 64 MiB of HBM per device.

v0:
```python
import jax
import jax.numpy as jnp
from jax import lax
from jax.sharding import PartitionSpec as P

PRE_SWEEPS = 2
COARSE_SWEEPS = 4


relaxation = 0.8
highest = lax.Precision.HIGHEST


def with_halo(block, sides, width):
    for axis, dim in sides:
        count = lax.axis_size(axis)
        forward = [(i, i + 1) for i in range(count - 1)]
        backward = [(target, source) for source, target in forward]
        low = lax.ppermute(
            lax.slice_in_dim(block, block.shape[dim] - width, None, axis=dim), axis, forward
        )
        high = lax.ppermute(lax.slice_in_dim(block, 0, width, axis=dim), axis, backward)
        block = jnp.concatenate([low, block, high], axis=dim)
    return block


def face_stack(field):
    cubes = field.reshape(-1, 16, 16, 16)
    layers = [
        cubes[:, 0],
        cubes[:, -1],
        cubes[:, :, 0],
        cubes[:, :, -1],
        cubes[:, :, :, 0],
        cubes[:, :, :, -1],
    ]
    return jnp.stack(layers, axis=1).reshape(-1, 6, 256)


def apply_operator(field, ghosts, coefficient):
    cubes = field.reshape(-1, 16, 16, 16)
    sides = ghosts.reshape(-1, 6, 16, 16)
    x_plus = jnp.concatenate([cubes[:, 1:], sides[:, 1][:, None]], axis=1)
    x_minus = jnp.concatenate([sides[:, 0][:, None], cubes[:, :-1]], axis=1)
    y_plus = jnp.concatenate([cubes[:, :, 1:], sides[:, 3][:, :, None]], axis=2)
    y_minus = jnp.concatenate([sides[:, 2][:, :, None], cubes[:, :, :-1]], axis=2)
    z_plus = jnp.concatenate([cubes[:, :, :, 1:], sides[:, 5][:, :, :, None]], axis=3)
    z_minus = jnp.concatenate([sides[:, 4][:, :, :, None], cubes[:, :, :, :-1]], axis=3)
    beside = x_plus + x_minus
    beside = beside + y_plus + y_minus
    beside = beside + z_plus + z_minus
    return (6.0 + coefficient) * field - beside.reshape(-1, 4096)


def select_faces(links, window, base):
    columns = jnp.arange(window.shape[0], dtype=jnp.int32)
    local_links = links - base
    selector = (
        (local_links[:, :, None] == columns[None, None, :]) & (links >= 0)[:, :, None]
    ).astype(jnp.float32)
    return jnp.einsum("bdw,wdx->bdx", selector, window, precision=highest)


def ghost_layers(field, face_links):
    faces = face_stack(field)
    flipped = jnp.array([1, 0, 3, 2, 5, 4], dtype=jnp.int32)
    ranged = lax.all_gather(faces, "sub", axis=0, tiled=True)
    window = with_halo(ranged, (("curve", 0),), ranged.shape[0])
    span = window.shape[0] // 3
    return select_faces(face_links, window[:, flipped], (lax.axis_index("curve") - 1) * span)


def sweep(field, source, coefficient, face_links):
    image = apply_operator(field, ghost_layers(field, face_links), coefficient)
    return field + relaxation * (source - image) / (6.0 + coefficient)


def near_errors(block_error):
    ranged = lax.all_gather(block_error, "sub", axis=0, tiled=True)
    window = with_halo(ranged, (("curve", 0),), ranged.shape[0])
    return window


def window_sum(window, face_links):
    span = window.shape[0] // 3
    base = (lax.axis_index("curve") - 1) * span
    local_links = face_links - base
    clipped = jnp.clip(local_links, 0, window.shape[0] - 1)
    return jnp.sum(jnp.where(face_links >= 0, window[clipped], 0.0), axis=1)


def earlier_same(targets):
    same_target = (targets[..., :, None] == targets[..., None, :]).astype(jnp.int32)
    return jnp.sum(jnp.tril(same_target, -1), axis=-1)


def on_device(pressure, source_term, coefficient, new_slot, face_links):
    blocks_here = pressure.shape[0]
    nsub = lax.axis_size("sub")
    most = max(1, blocks_here // nsub)
    own_sub = lax.axis_index("sub")
    all_slots = lax.all_gather(new_slot, "sub", axis=0, tiled=True).reshape(nsub, blocks_here)
    target_dev = new_slot // blocks_here
    order_rank = earlier_same(target_dev)
    peers = jnp.arange(nsub, dtype=jnp.int32)
    places = jnp.arange(most, dtype=jnp.int32)
    send_sel = (
        (target_dev[None, None, :] == peers[:, None, None])
        & (order_rank[None, None, :] == places[None, :, None])
    ).astype(jnp.float32)
    stacked = jnp.stack([pressure, source_term, coefficient], axis=1)
    outgoing = jnp.einsum("qmj,jcx->qmcx", send_sel, stacked, precision=highest)
    incoming = lax.all_to_all(outgoing, "sub", split_axis=0, concat_axis=0, tiled=True)
    all_targets = all_slots // blocks_here
    all_ranks = earlier_same(all_targets)
    all_places = all_slots % blocks_here
    arrivals = all_targets == own_sub
    slots_here = jnp.arange(blocks_here, dtype=jnp.int32)
    matched = (
        arrivals[None, :, :, None]
        & (all_places[None, :, :, None] == slots_here[:, None, None, None])
        & (all_ranks[None, :, :, None] == places[None, None, None, :])
    )
    recv_sel = jnp.sum(matched.astype(jnp.float32), axis=2)
    moved = jnp.einsum("kpm,pmcx->kcx", recv_sel, incoming, precision=highest)
    moved_p = moved[:, 0]
    moved_f = moved[:, 1]
    moved_c = moved[:, 2]
    smoothed = moved_p
    for step in range(PRE_SWEEPS):
        smoothed = sweep(smoothed, moved_f, moved_c, face_links)
    residual = moved_f - apply_operator(smoothed, ghost_layers(smoothed, face_links), moved_c)
    block_residual = jnp.mean(residual, axis=1)
    block_diag = 6.0 + jnp.mean(moved_c, axis=1)
    block_error = jnp.zeros((blocks_here,), jnp.float32)
    for step in range(COARSE_SWEEPS):
        if step == 0:
            beside = jnp.zeros((blocks_here,), jnp.float32)
        else:
            beside = window_sum(near_errors(block_error), face_links)
        block_error = (
            block_error
            + relaxation * (block_residual - block_diag * block_error + beside) / block_diag
        )
    lifted = smoothed + block_error[:, None]
    return sweep(lifted, moved_f, moved_c, face_links)


def solution(mesh):
    placed = (
        P(("curve", "sub"), None),
        P(("curve", "sub"), None),
        P(("curve", "sub"), None),
        P(("curve", "sub")),
        P(("curve", "sub"), None),
    )
    return jax.shard_map(
        on_device, mesh=mesh, in_specs=placed, out_specs=P(("curve", "sub"), None), check_vma=False
    )
```

profile of v0, /device:TPU:0, one launch (start us, length us, event | category | flops | bytes accessed | tf_op | source)
XLA Modules:
  0.0 139.6 jit_solution(7166398245080115785)
XLA Ops:
  0.9 2.0 %fusion.16 = f32[2,2,3,4096]{3,1,2,0:T(2,128)} fusion(f32[4,1,4096]{2,0,1:T(4,128)} %bitcast.233, f32[4,1,4096]{2,0,1:T(4,128)} %bitcast.234, f32[4,1,4096]{2,0,1:T(4,128)} %bitcast.235, pred[2,2,4,1]{2,0,1,3:T(4,128)(4,1)S(1)} %and_bitcast_fusion), kind=kOutput, calls=%fused_computation.36 | convolution fusion | flops 2457600 | bytes 393232 | tf_op jit(solution)/shard_map/qmj,jcx->qmcx/dot_general | solution.py:112
  2.8 3.4 %all-to-all-start = ((f32[2,2,3,4096]{3,1,2,0:T(2,128)}), f32[2,2,3,4096]{3,1,2,0:T(2,128)S(1)}, u32[]{:S(2)}, u32[]{:S(2)}) async-start(f32[2,2,3,4096]{3,1,2,0:T(2,128)} %fusion.16), calls=%async_computation | async-start | bytes 393216 | tf_op jit(solution)/shard_map/all_to_all | solution.py:113
  9.1 1.9 %all-reduce = s32[8]{0:T(128)S(1)} all-reduce(s32[8]{0:T(128)S(1)} %dynamic-update-slice), channel_id=1, replica_groups=mesh['curve'=16,'sub'=2] {'sub'}, use_global_device_ids=true, to_apply=%add | all-reduce | flops 8 | bytes 64
  14.3 1.9 %all_gather.25 = f32[8,6,256]{2,1,0:T(8,128)S(1)} all-gather(f32[4,6,256]{2,1,0:T(8,128)S(1)} %copy.216), channel_id=1, replica_groups=mesh['curve'=16,'sub'=2] {'sub'}, dimensions={0}, use_global_device_ids=true | all-gather | bytes 73728 | tf_op jit(solution)/shard_map/all_gather | solution.py:67
  16.2 4.8 %collective-permute-start = (f32[8,6,256]{2,0,1:T(8,128)S(1)}, f32[8,6,256]{2,0,1:T(8,128)S(1)}, u32[]{:S(2)}, u32[]{:S(2)}) collective-permute-start(f32[8,6,256]{2,0,1:T(8,128)S(1)} %copy.217), channel_id=1, source_target_pairs={{0,2},{2,4},{4,6},{6,8},{8,10},{10,12},{12,14},{14,16},{16,18},{18... | collective-permute-start | bytes 147464 | tf_op jit(solution)/shard_map/ppermute | solution.py:19
  21.0 1.3 collective-permute-start.1
  29.6 1.3 copy.228
  31.1 2.7 %divide_add_fusion.1 = (f32[4,16,16,16]{2,1,0,3:T(8,128)S(1)}, f32[4,16,16,16]{2,1,0,3:T(8,128)S(1)}) fusion(f32[4,16,16,16]{2,1,0,3:T(8,128)S(1)} %copy.213, f32[4,16,16,16]{2,1,0,3:T(8,128)S(1)} %copy.232, f32[4,16,16,16]{2,1,0,3:T(8,128)S(1)} %copy.234, f32[4,16,16,15]{2,1,0,3:T(8,128)} %get-tuple-element.64, f32[4,16,16,1]{2,1,0,3:T(8,128)S(1)} %get-tuple-element.92, ...), kind=kLoop, calls=%fused_computation.33 | loop fusion | flops 278528 | bytes 720896 | tf_op jit(solution)/shard_map/add | solution.py:75
  35.8 1.9 %all_gather.26 = f32[8,6,256]{2,1,0:T(8,128)S(1)} all-gather(f32[4,6,256]{2,1,0:T(8,128)S(1)} %copy.241), channel_id=1, replica_groups=mesh['curve'=16,'sub'=2] {'sub'}, dimensions={0}, use_global_device_ids=true | all-gather | bytes 73728 | tf_op jit(solution)/shard_map/all_gather | solution.py:67
  37.6 4.5 %collective-permute-start.2 = (f32[8,6,256]{2,0,1:T(8,128)S(1)}, f32[8,6,256]{2,0,1:T(8,128)S(1)}, u32[]{:S(2)}, u32[]{:S(2)}) collective-permute-start(f32[8,6,256]{2,0,1:T(8,128)S(1)} %copy.242), channel_id=1, source_target_pairs={{0,2},{2,4},{4,6},{6,8},{8,10},{10,12},{12,14},{14,16},{16,18},{18... | collective-permute-start | bytes 147464 | tf_op jit(solution)/shard_map/ppermute | solution.py:19
  50.1 1.4 copy.248
  51.6 2.7 %divide_add_fusion = (f32[4,16,16,16]{2,1,0,3:T(8,128)S(1)}, f32[4,16,16,16]{2,1,0,3:T(8,128)S(1)}) fusion(f32[4,16,16,16]{2,1,0,3:T(8,128)S(1)} %get-tuple-element.19, f32[4,16,16,16]{2,1,0,3:T(8,128)S(1)} %copy.232, f32[4,16,16,16]{2,1,0,3:T(8,128)S(1)} %copy.234, f32[4,16,16,15]{2,1,0,3:T(8,128)} %get-tuple-element.52, ...), kind=kLoop, calls=%fused_computation.32 | loop fusion | flops 278528 | bytes 720896 | tf_op jit(solution)/shard_map/add | solution.py:75
  56.3 1.9 %all_gather.27 = f32[8,6,256]{2,1,0:T(8,128)S(1)} all-gather(f32[4,6,256]{2,1,0:T(8,128)S(1)} %copy.257), channel_id=1, replica_groups=mesh['curve'=16,'sub'=2] {'sub'}, dimensions={0}, use_global_device_ids=true | all-gather | bytes 73728 | tf_op jit(solution)/shard_map/all_gather | solution.py:67
  58.2 4.8 %collective-permute-start.4 = (f32[8,6,256]{2,0,1:T(8,128)S(1)}, f32[8,6,256]{2,0,1:T(8,128)S(1)}, u32[]{:S(2)}, u32[]{:S(2)}) collective-permute-start(f32[8,6,256]{2,0,1:T(8,128)S(1)} %copy.258), channel_id=1, source_target_pairs={{0,2},{2,4},{4,6},{6,8},{8,10},{10,12},{12,14},{14,16},{16,18},{18... | collective-permute-start | bytes 147464 | tf_op jit(solution)/shard_map/ppermute | solution.py:19
  63.0 1.5 %collective-permute-start.5 = (f32[8,6,256]{2,0,1:T(8,128)S(1)}, f32[8,6,256]{2,0,1:T(8,128)S(1)}, u32[]{:S(2)}, u32[]{:S(2)}) collective-permute-start(f32[8,6,256]{2,0,1:T(8,128)S(1)} %copy.258), channel_id=1, source_target_pairs={{2,0},{4,2},{6,4},{8,6},{10,8},{12,10},{14,12},{16,14},{18,16},{20... | collective-permute-start | bytes 147464 | tf_op jit(solution)/shard_map/ppermute | solution.py:22
  67.4 1.5 %collective-permute-done.5 = f32[8,6,256]{2,0,1:T(8,128)S(1)} collective-permute-done((f32[8,6,256]{2,0,1:T(8,128)S(1)}, f32[8,6,256]{2,0,1:T(8,128)S(1)}, u32[]{:S(2)}, u32[]{:S(2)}) %collective-permute-start.5) | collective-permute-done | bytes 49184 | tf_op jit(solution)/shard_map/ppermute | solution.py:22
  72.7 2.0 %fusion.11 = f32[4,16,16,16]{2,1,0,3:T(8,128)S(1)} fusion(f32[4,1,16,16]{2,1,0,3:T(1,128)} %copy.261, f32[4,15,16,16]{2,1,0,3:T(8,128)} %get-tuple-element.40, f32[4,15,16,16]{2,1,0,3:T(8,128)} %get-tuple-element.39, f32[4,1,16,16]{2,1,0,3:T(1,128)} %copy.262, f32[4,16,1,16]{2,1,0,3:T(8,128)S(1)} %copy.263, f32[4,16,15,16]{2,1,0,3:T(8,128)S(1)} %get-tuple-element.38, ...), kind=kLoop, calls=%fused_computation.26 | loop fusion | flops 180224 | bytes 458752 | tf_op jit(solution)/shard_map/add | solution.py:51
  76.2 2.4 %all-reduce.1 = f32[8]{0:T(128)S(1)} all-reduce(f32[8]{0:T(128)S(1)} %get-tuple-element.13), channel_id=1, replica_groups=mesh['curve'=16,'sub'=2] {'sub'}, use_global_device_ids=true, to_apply=%add.1 | all-reduce | flops 8 | bytes 64
  78.7 4.7 %collective-permute-start.6 = (f32[8]{0:T(128)S(1)}, f32[8]{0:T(128)S(1)}, u32[]{:S(2)}, u32[]{:S(2)}) collective-permute-start(f32[8]{0:T(128)S(1)} %all-reduce.1), channel_id=1, source_target_pairs={{0,2},{2,4},{4,6},{6,8},{8,10},{10,12},{12,14},{14,16},{16,18},{18... | collective-permute-start | bytes 104 | tf_op jit(solution)/shard_map/ppermute | solution.py:19
  83.3 1.3 collective-permute-start.7
  84.6 4.1 %collective-permute-done.7 = f32[8]{0:T(128)S(1)} collective-permute-done((f32[8]{0:T(128)S(1)}, f32[8]{0:T(128)S(1)}, u32[]{:S(2)}, u32[]{:S(2)}) %collective-permute-start.7) | collective-permute-done | bytes 64 | tf_op jit(solution)/shard_map/ppermute | solution.py:22
  89.9 2.4 %all-reduce.2 = f32[8]{0:T(128)S(1)} all-reduce(f32[8]{0:T(128)S(1)} %get-tuple-element.9), channel_id=1, replica_groups=mesh['curve'=16,'sub'=2] {'sub'}, use_global_device_ids=true, to_apply=%add.2 | all-reduce | flops 8 | bytes 64
  92.3 5.5 %collective-permute-start.8 = (f32[8]{0:T(128)S(1)}, f32[8]{0:T(128)S(1)}, u32[]{:S(2)}, u32[]{:S(2)}) collective-permute-start(f32[8]{0:T(128)S(1)} %all-reduce.2), channel_id=1, source_target_pairs={{0,2},{2,4},{4,6},{6,8},{8,10},{10,12},{12,14},{14,16},{16,18},{18... | collective-permute-start | bytes 104 | tf_op jit(solution)/shard_map/ppermute | solution.py:19
  99.1 4.1 %collective-permute-done.9 = f32[8]{0:T(128)S(1)} collective-permute-done((f32[8]{0:T(128)S(1)}, f32[8]{0:T(128)S(1)}, u32[]{:S(2)}, u32[]{:S(2)}) %collective-permute-start.9) | collective-permute-done | bytes 64 | tf_op jit(solution)/shard_map/ppermute | solution.py:22
  104.4 2.4 %all-reduce.3 = f32[8]{0:T(128)S(1)} all-reduce(f32[8]{0:T(128)S(1)} %get-tuple-element.7), channel_id=1, replica_groups=mesh['curve'=16,'sub'=2] {'sub'}, use_global_device_ids=true, to_apply=%add.3 | all-reduce | flops 8 | bytes 64
  106.8 4.8 %collective-permute-start.10 = (f32[8]{0:T(128)S(1)}, f32[8]{0:T(128)S(1)}, u32[]{:S(2)}, u32[]{:S(2)}) collective-permute-start(f32[8]{0:T(128)S(1)} %all-reduce.3), channel_id=1, source_target_pairs={{0,2},{2,4},{4,6},{6,8},{8,10},{10,12},{12,14},{14,16},{16,18},{18... | collective-permute-start | bytes 104 | tf_op jit(solution)/shard_map/ppermute | solution.py:19
  111.6 1.3 collective-permute-start.11
  112.9 4.1 %collective-permute-done.11 = f32[8]{0:T(128)S(1)} collective-permute-done((f32[8]{0:T(128)S(1)}, f32[8]{0:T(128)S(1)}, u32[]{:S(2)}, u32[]{:S(2)}) %collective-permute-start.11) | collective-permute-done | bytes 64 | tf_op jit(solution)/shard_map/ppermute | solution.py:22
  120.6 1.9 %all_gather.31 = f32[8,6,256]{2,1,0:T(8,128)S(1)} all-gather(f32[4,6,256]{2,1,0:T(8,128)S(1)} %copy.270), channel_id=1, replica_groups=mesh['curve'=16,'sub'=2] {'sub'}, dimensions={0}, use_global_device_ids=true | all-gather | bytes 73728 | tf_op jit(solution)/shard_map/all_gather | solution.py:67
  122.5 4.8 %collective-permute-start.12 = (f32[8,6,256]{2,0,1:T(8,128)S(1)}, f32[8,6,256]{2,0,1:T(8,128)S(1)}, u32[]{:S(2)}, u32[]{:S(2)}) collective-permute-start(f32[8,6,256]{2,0,1:T(8,128)S(1)} %copy.271), channel_id=1, source_target_pairs={{0,2},{2,4},{4,6},{6,8},{8,10},{10,12},{12,14},{14,16},{16,18},{18... | collective-permute-start | bytes 147464 | tf_op jit(solution)/shard_map/ppermute | solution.py:19
  130.8 2.5 %collective-permute-done.13 = f32[8,6,256]{2,0,1:T(8,128)S(1)} collective-permute-done((f32[8,6,256]{2,0,1:T(8,128)S(1)}, f32[8,6,256]{2,0,1:T(8,128)S(1)}, u32[]{:S(2)}, u32[]{:S(2)}) %collective-permute-start.13) | collective-permute-done | bytes 49184 | tf_op jit(solution)/shard_map/ppermute | solution.py:22
  135.7 1.9 %fusion.15 = f32[4,16,16,16]{2,1,0,3:T(8,128)S(1)} fusion(f32[4,1,16,16]{2,1,0,3:T(1,128)S(1)} %copy.274, f32[4,15,16,16]{2,1,0,3:T(8,128)} %get-tuple-element.28, f32[4,15,16,16]{2,1,0,3:T(8,128)S(1)} %get-tuple-element.27, f32[4,1,16,16]{2,1,0,3:T(1,128)S(1)} %copy.275, f32[4,16,1,16]{2,1,0,3:T(8,128)S(1)} %copy.276, ...), kind=kLoop, calls=%fused_computation.31 | loop fusion | flops 180224 | bytes 458752 | tf_op jit(solution)/shard_map/add | solution.py:51
  (216 shorter events, 48.4 us)
Async XLA Ops:
  2.8 8.6 %all-to-all-start = ((f32[2,2,3,4096]{3,1,2,0:T(2,128)}), f32[2,2,3,4096]{3,1,2,0:T(2,128)S(1)}, u32[]{:S(2)}, u32[]{:S(2)}) async-start(f32[2,2,3,4096]{3,1,2,0:T(2,128)} %fusion.16), calls=%async_computation | async-start | bytes 393216 | tf_op jit(solution)/shard_map/all_to_all | solution.py:113
  6.3 0.7 copy-start.7
  8.2 0.7 copy-start.6
  16.2 11.9 %collective-permute-start = (f32[8,6,256]{2,0,1:T(8,128)S(1)}, f32[8,6,256]{2,0,1:T(8,128)S(1)}, u32[]{:S(2)}, u32[]{:S(2)}) collective-permute-start(f32[8,6,256]{2,0,1:T(8,128)S(1)} %copy.217), channel_id=1, source_target_pairs={{0,2},{2,4},{4,6},{6,8},{8,10},{10,12},{12,14},{14,16},{16,18},{18... | collective-permute-start | bytes 147464 | tf_op jit(solution)/shard_map/ppermute | solution.py:19
  21.0 7.0 %collective-permute-start.1 = (f32[8,6,256]{2,0,1:T(8,128)S(1)}, f32[8,6,256]{2,0,1:T(8,128)S(1)}, u32[]{:S(2)}, u32[]{:S(2)}) collective-permute-start(f32[8,6,256]{2,0,1:T(8,128)S(1)} %copy.217), channel_id=1, source_target_pairs={{2,0},{4,2},{6,4},{8,6},{10,8},{12,10},{14,12},{16,14},{18,16},{20... | collective-permute-start | bytes 147464 | tf_op jit(solution)/shard_map/ppermute | solution.py:22
  24.5 1.1 copy-start.5
  25.6 22.9 %copy-start.2 = (s32[1024]{0:T(1024)}, s32[1024]{0:T(1024)S(1)}, u32[]{:S(2)}) copy-start(s32[1024]{0:T(1024)S(1)} %pad_clamp_fusion.1) | copy-start | bytes 12292
  25.6 0.7 copy-start
  37.6 9.7 %collective-permute-start.2 = (f32[8,6,256]{2,0,1:T(8,128)S(1)}, f32[8,6,256]{2,0,1:T(8,128)S(1)}, u32[]{:S(2)}, u32[]{:S(2)}) collective-permute-start(f32[8,6,256]{2,0,1:T(8,128)S(1)} %copy.242), channel_id=1, source_target_pairs={{0,2},{2,4},{4,6},{6,8},{8,10},{10,12},{12,14},{14,16},{16,18},{18... | collective-permute-start | bytes 147464 | tf_op jit(solution)/shard_map/ppermute | solution.py:19
  42.2 6.4 %collective-permute-start.3 = (f32[8,6,256]{2,0,1:T(8,128)S(1)}, f32[8,6,256]{2,0,1:T(8,128)S(1)}, u32[]{:S(2)}, u32[]{:S(2)}) collective-permute-start(f32[8,6,256]{2,0,1:T(8,128)S(1)} %copy.242), channel_id=1, source_target_pairs={{2,0},{4,2},{6,4},{8,6},{10,8},{12,10},{14,12},{16,14},{18,16},{20... | collective-permute-start | bytes 147464 | tf_op jit(solution)/shard_map/ppermute | solution.py:22
  58.2 9.3 %collective-permute-start.4 = (f32[8,6,256]{2,0,1:T(8,128)S(1)}, f32[8,6,256]{2,0,1:T(8,128)S(1)}, u32[]{:S(2)}, u32[]{:S(2)}) collective-permute-start(f32[8,6,256]{2,0,1:T(8,128)S(1)} %copy.258), channel_id=1, source_target_pairs={{0,2},{2,4},{4,6},{6,8},{8,10},{10,12},{12,14},{14,16},{16,18},{18... | collective-permute-start | bytes 147464 | tf_op jit(solution)/shard_map/ppermute | solution.py:19
  63.0 6.0 %collective-permute-start.5 = (f32[8,6,256]{2,0,1:T(8,128)S(1)}, f32[8,6,256]{2,0,1:T(8,128)S(1)}, u32[]{:S(2)}, u32[]{:S(2)}) collective-permute-start(f32[8,6,256]{2,0,1:T(8,128)S(1)} %copy.258), channel_id=1, source_target_pairs={{2,0},{4,2},{6,4},{8,6},{10,8},{12,10},{14,12},{16,14},{18,16},{20... | collective-permute-start | bytes 147464 | tf_op jit(solution)/shard_map/ppermute | solution.py:22
  75.5 0.6 copy-start.1
  78.7 6.0 %collective-permute-start.6 = (f32[8]{0:T(128)S(1)}, f32[8]{0:T(128)S(1)}, u32[]{:S(2)}, u32[]{:S(2)}) collective-permute-start(f32[8]{0:T(128)S(1)} %all-reduce.1), channel_id=1, source_target_pairs={{0,2},{2,4},{4,6},{6,8},{8,10},{10,12},{12,14},{14,16},{16,18},{18... | collective-permute-start | bytes 104 | tf_op jit(solution)/shard_map/ppermute | solution.py:19
  83.3 5.4 %collective-permute-start.7 = (f32[8]{0:T(128)S(1)}, f32[8]{0:T(128)S(1)}, u32[]{:S(2)}, u32[]{:S(2)}) collective-permute-start(f32[8]{0:T(128)S(1)} %all-reduce.1), channel_id=1, source_target_pairs={{2,0},{4,2},{6,4},{8,6},{10,8},{12,10},{14,12},{16,14},{18,16},{20... | collective-permute-start | bytes 104 | tf_op jit(solution)/shard_map/ppermute | solution.py:22
  92.3 6.8 %collective-permute-start.8 = (f32[8]{0:T(128)S(1)}, f32[8]{0:T(128)S(1)}, u32[]{:S(2)}, u32[]{:S(2)}) collective-permute-start(f32[8]{0:T(128)S(1)} %all-reduce.2), channel_id=1, source_target_pairs={{0,2},{2,4},{4,6},{6,8},{8,10},{10,12},{12,14},{14,16},{16,18},{18... | collective-permute-start | bytes 104 | tf_op jit(solution)/shard_map/ppermute | solution.py:19
  97.8 5.4 %collective-permute-start.9 = (f32[8]{0:T(128)S(1)}, f32[8]{0:T(128)S(1)}, u32[]{:S(2)}, u32[]{:S(2)}) collective-permute-start(f32[8]{0:T(128)S(1)} %all-reduce.2), channel_id=1, source_target_pairs={{2,0},{4,2},{6,4},{8,6},{10,8},{12,10},{14,12},{16,14},{18,16},{20... | collective-permute-start | bytes 104 | tf_op jit(solution)/shard_map/ppermute | solution.py:22
  106.8 6.1 %collective-permute-start.10 = (f32[8]{0:T(128)S(1)}, f32[8]{0:T(128)S(1)}, u32[]{:S(2)}, u32[]{:S(2)}) collective-permute-start(f32[8]{0:T(128)S(1)} %all-reduce.3), channel_id=1, source_target_pairs={{0,2},{2,4},{4,6},{6,8},{8,10},{10,12},{12,14},{14,16},{16,18},{18... | collective-permute-start | bytes 104 | tf_op jit(solution)/shard_map/ppermute | solution.py:19
  111.6 5.4 %collective-permute-start.11 = (f32[8]{0:T(128)S(1)}, f32[8]{0:T(128)S(1)}, u32[]{:S(2)}, u32[]{:S(2)}) collective-permute-start(f32[8]{0:T(128)S(1)} %all-reduce.3), channel_id=1, source_target_pairs={{2,0},{4,2},{6,4},{8,6},{10,8},{12,10},{14,12},{16,14},{18,16},{20... | collective-permute-start | bytes 104 | tf_op jit(solution)/shard_map/ppermute | solution.py:22
  118.1 0.5 copy-start.3
  122.5 8.3 %collective-permute-start.12 = (f32[8,6,256]{2,0,1:T(8,128)S(1)}, f32[8,6,256]{2,0,1:T(8,128)S(1)}, u32[]{:S(2)}, u32[]{:S(2)}) collective-permute-start(f32[8,6,256]{2,0,1:T(8,128)S(1)} %copy.271), channel_id=1, source_target_pairs={{0,2},{2,4},{4,6},{6,8},{8,10},{10,12},{12,14},{14,16},{16,18},{18... | collective-permute-start | bytes 147464 | tf_op jit(solution)/shard_map/ppermute | solution.py:19
  127.3 6.0 %collective-permute-start.13 = (f32[8,6,256]{2,0,1:T(8,128)S(1)}, f32[8,6,256]{2,0,1:T(8,128)S(1)}, u32[]{:S(2)}, u32[]{:S(2)}) collective-permute-start(f32[8,6,256]{2,0,1:T(8,128)S(1)} %copy.271), channel_id=1, source_target_pairs={{2,0},{4,2},{6,4},{8,6},{10,8},{12,10},{14,12},{16,14},{18,16},{20... | collective-permute-start | bytes 147464 | tf_op jit(solution)/shard_map/ppermute | solution.py:22
  138.2 0.7 copy-start.4
where the time goes:
time: 140 us
  starting transfers between devices  46.7 us (33%)
  local copies, waits for them, and re-layouts  40.4 us (29%)
  waiting for transfers between devices  17.7 us (13%)
  blocking collectives  16.7 us (12%)
  other arithmetic  13.2 us (9%)
  matrix products  3.45 us (2%)
  between operations  1.46 us (1%)
    ppermute x7, starting transfers between devices, with_halo(): lax.ppermute(lax.slice_in_dim(block, block.shape[dim] - width, None, axis...  34 us
    ppermute x7, waiting for transfers between devices, with_halo(): lax.ppermute(lax.slice_in_dim(block, 0, width, axis=dim), axis, backward)  17.6 us
    unnamed x4, blocking collectives  9.29 us
    ppermute x7, starting transfers between devices, with_halo(): lax.ppermute(lax.slice_in_dim(block, 0, width, axis=dim), axis, backward)  9.23 us
    all_gather x4, blocking collectives, ghost_layers(): ranged = lax.all_gather(faces, 'sub', axis=0, tiled=True)  7.42 us
    add x3, other arithmetic, sweep(): return field + relaxation * (source - image) / (6.0 + coefficient)  6.04 us
    unnamed x42, local copies, waits for them, and re-layouts  4.56 us
    add x2, other arithmetic, apply_operator(): beside = beside + z_plus + z_minus  3.9 us
  transfers between devices with their start and end apart: 15, of which 6 were waited for; matrix products, arithmetic and copies ran while one was open for 11% of the time, Pallas kernels for 0%

commit v1 on v0

v1 whole, which is shorter than its diff:
```python
import functools

import jax
import jax.numpy as jnp
from jax import lax
from jax.experimental import pallas as pl
from jax.experimental.pallas import tpu as pltpu
from jax.sharding import PartitionSpec as P

PRE_SWEEPS = 2
COARSE_SWEEPS = 4
SIDE = 16
FACE = SIDE * SIDE
FACES = 6
LANES = 128
FLIP = (1, 0, 3, 2, 5, 4)

relaxation = 0.8
MESH = pl.DeviceIdType.MESH


def kernel(
    count,
    nsub,
    blocks,
    slot_ref,
    link_ref,
    p_ref,
    f_ref,
    c_ref,
    out_ref,
    raw,
    first,
    window_a,
    window_b,
    ghosts,
    peer_p,
    peer_f,
    peer_c,
    mf,
    mc,
    inv,
    u_a,
    u_b,
    base,
    coarse,
    raw_send,
    raw_recv,
    face_send,
    face_recv,
    peer_send,
    peer_recv,
    coarse_send,
    coarse_recv,
):
    pos = lax.axis_index("curve")
    sub = lax.axis_index("sub")
    group = nsub * blocks
    reach = COARSE_SWEEPS
    wall = 3 * nsub
    windows = (window_a, window_b)

    def partners(radius):
        for t in range(-radius, radius + 1):
            for ds in range(nsub):
                if t or ds:
                    yield t, lax.rem(sub + ds, nsub)

    def guarded(t, action):
        if t == 0:
            action()
        else:
            there = pos + t
            pl.when((there >= 0) & (there < count))(action)

    for window in (first, *windows):
        window[wall] = jnp.zeros(window.shape[1:], jnp.float32)
        for t in (-1, 1):

            @pl.when((pos + t < 0) | (pos + t >= count))
            def _(window=window, t=t):
                for s in range(nsub):
                    window[(t + 1) * nsub + s] = jnp.zeros(window.shape[1:], jnp.float32)

    for t in (-1, 1):

        @pl.when((pos + t < 0) | (pos + t >= count))
        def _(t=t):
            for s in range(nsub):
                raw[(t + 1) * nsub + s] = jnp.zeros(raw.shape[1:], jnp.float32)

    for t in range(-reach, reach + 1):
        if t:

            @pl.when((pos + t < 0) | (pos + t >= count))
            def _(t=t):
                for s in range(nsub):
                    coarse[(t + reach) * nsub + s] = jnp.zeros(coarse.shape[1:], jnp.float32)

    barrier = pltpu.get_barrier_semaphore()
    for t, s in partners(reach):

        def greet(t=t, s=s):
            pl.semaphore_signal(barrier, inc=1, device_id=(pos + t, s), device_id_type=MESH)

        guarded(t, greet)
    low = jnp.minimum(pos, reach)
    high = jnp.minimum(count - 1 - pos, reach)
    pl.semaphore_wait(barrier, (low + high + 1) * nsub - 1)

    def descriptor(source, window, sends, recvs, radius, t, s):
        slot = (radius - t) * nsub + sub
        return pltpu.make_async_remote_copy(
            src_ref=source,
            dst_ref=window.at[slot],
            send_sem=sends.at[(t + radius) * nsub + s],
            recv_sem=recvs.at[slot],
            device_id=(pos + t, s),
            device_id_type=MESH,
        )

    def send_all(window, sends, recvs, radius):
        own = window.at[radius * nsub + sub]
        for t, s in partners(radius):

            def go(t=t, s=s):
                descriptor(own, window, sends, recvs, radius, t, s).start()

            guarded(t, go)

    def wait_all(window, sends, recvs, radius):
        own = window.at[radius * nsub + sub]
        for t, s in partners(radius):

            def hold(t=t, s=s):
                slot = (t + radius) * nsub + s
                pltpu.make_async_remote_copy(
                    src_ref=own,
                    dst_ref=window.at[slot],
                    send_sem=sends.at[slot],
                    recv_sem=recvs.at[slot],
                    device_id=(pos + t, s),
                    device_id_type=MESH,
                ).wait_recv()

            guarded(t, hold)

    def wait_sends(window, sends, recvs, radius):
        own = window.at[radius * nsub + sub]
        for t, s in partners(radius):

            def hold(t=t, s=s):
                descriptor(own, window, sends, recvs, radius, t, s).wait_send()

            guarded(t, hold)

    lane = lax.broadcasted_iota(jnp.int32, (blocks, FACE), 1)
    strip = lane // SIDE
    within = lane % SIDE

    def pack(field, target, lead):
        def column(x):
            return field[:, x * FACE : (x + 1) * FACE]

        target[lead, :, 0:FACE] = column(0)
        target[lead, :, FACE : 2 * FACE] = column(SIDE - 1)
        y_low = y_high = z_low = z_high = jnp.zeros((blocks, FACE), jnp.float32)
        for x in range(SIDE):
            part = column(x)
            y_low = jnp.where(strip == x, pltpu.roll(part, SIDE * x, 1), y_low)
            y_high = jnp.where(strip == x, pltpu.roll(part, (SIDE * (x + 1)) % FACE, 1), y_high)
            z_low = jnp.where(within == x, pltpu.roll(part, x, 1), z_low)
            z_high = jnp.where(within == x, pltpu.roll(part, (x - SIDE + 1) % FACE, 1), z_high)
        target[lead, :, 2 * FACE : 3 * FACE] = y_low
        target[lead, :, 3 * FACE : 4 * FACE] = y_high
        target[lead, :, 4 * FACE : 5 * FACE] = z_low
        target[lead, :, 5 * FACE : 6 * FACE] = z_high

    peers = []
    for ds in range(1, nsub):
        there = lax.rem(sub + ds, nsub)
        for k, (source, landing) in enumerate(((p_ref, peer_p), (f_ref, peer_f), (c_ref, peer_c))):
            copy = pltpu.make_async_remote_copy(
                src_ref=source,
                dst_ref=landing.at[nsub - ds - 1],
                send_sem=peer_send.at[k, ds - 1],
                recv_sem=peer_recv.at[k, nsub - ds - 1],
                device_id=(pos, there),
                device_id_type=MESH,
            )
            peers.append((ds, k, landing, copy))

    own_slot = nsub + sub
    pack(p_ref, raw, own_slot)
    row = lax.broadcasted_iota(jnp.int32, (blocks, LANES), 0)
    slots = jnp.zeros((blocks, LANES), jnp.int32)
    for j in range(blocks):
        slots = jnp.where(row == j, slot_ref[j], slots)
    raw[own_slot, :, FACES * FACE :] = slots.astype(jnp.float32)
    send_all(raw, raw_send, raw_recv, 1)
    for _, _, _, copy in peers:
        copy.start()

    start = (pos - 1) * group
    places = []
    for b in range(blocks):
        for d in range(FACES):
            link = link_ref[b, d]
            offset = jnp.maximum(link - start, 0)
            places.append(
                (
                    b,
                    d,
                    jnp.where(link < 0, wall, offset // blocks),
                    jnp.where(link < 0, 0, offset % blocks),
                )
            )

    def gather(window):
        for b, d, device, place in places:
            flipped = FLIP[d]
            ghosts[d, pl.ds(b, 1), :] = window[
                device, pl.ds(place, 1), flipped * FACE : (flipped + 1) * FACE
            ]

    mine = (sub * blocks + row).astype(jnp.float32)

    def chosen(slot, j):
        return (raw[slot, j : j + 1, FACES * FACE :] == mine).astype(jnp.float32)

    def wide(select, length):
        return jnp.concatenate([select] * (length // LANES), axis=1)

    length = p_ref.shape[1]
    picks = [wide(chosen(own_slot, j), length) for j in range(blocks)]
    for source, target in ((p_ref, u_a), (f_ref, mf), (c_ref, mc)):
        total = picks[0] * source[0:1, :]
        for j in range(1, blocks):
            total = total + picks[j] * source[j : j + 1, :]
        target[...] = total

    wait_all(raw, raw_send, raw_recv, 1)

    group_row = lax.broadcasted_iota(jnp.int32, (group, LANES), 0).astype(jnp.float32)
    for t in range(3):
        total = jnp.zeros((group, FACES * FACE), jnp.float32)
        for s in range(nsub):
            slot = t * nsub + s
            for j in range(blocks):
                select = (raw[slot, j : j + 1, FACES * FACE :] == group_row).astype(jnp.float32)
                total = total + wide(select, FACES * FACE) * raw[slot, j : j + 1, : FACES * FACE]
        for s in range(nsub):
            first[t * nsub + s] = total[s * blocks : (s + 1) * blocks]
    gather(first)

    for ds in range(1, nsub):
        slot = nsub + lax.rem(sub + ds, nsub)
        picks = [wide(chosen(slot, j), length) for j in range(blocks)]
        for k, (landing, target) in enumerate(((peer_p, u_a), (peer_f, mf), (peer_c, mc))):
            pltpu.make_async_remote_copy(
                src_ref=p_ref,
                dst_ref=landing.at[ds - 1],
                send_sem=peer_send.at[k, ds - 1],
                recv_sem=peer_recv.at[k, ds - 1],
                device_id=(pos, lax.rem(sub + ds, nsub)),
                device_id_type=MESH,
            ).wait_recv()
            total = target[...]
            for j in range(blocks):
                total = total + picks[j] * landing[ds - 1, j : j + 1, :]
            target[...] = total

    inv[...] = relaxation / (6.0 + mc[...])

    def beside(field, x):
        def column(k):
            return field[:, k * FACE : (k + 1) * FACE]

        part = column(x)
        total = ghosts[0] if x == 0 else column(x - 1)
        total = total + (ghosts[1] if x == SIDE - 1 else column(x + 1))
        total = total + jnp.where(
            strip == 0,
            pltpu.roll(ghosts[2], (-SIDE * x) % FACE, 1),
            pltpu.roll(part, SIDE, 1),
        )
        total = total + jnp.where(
            strip == SIDE - 1,
            pltpu.roll(ghosts[3], SIDE * (SIDE - 1 - x), 1),
            pltpu.roll(part, FACE - SIDE, 1),
        )
        total = total + jnp.where(
            within == 0,
            pltpu.roll(ghosts[4], (-x) % FACE, 1),
            pltpu.roll(part, 1, 1),
        )
        total = total + jnp.where(
            within == SIDE - 1,
            pltpu.roll(ghosts[5], SIDE - 1 - x, 1),
            pltpu.roll(part, FACE - 1, 1),
        )
        return part, total

    def sweep(field, target):
        for x in range(SIDE):
            here = slice(x * FACE, (x + 1) * FACE)
            part, total = beside(field, x)
            target[:, here] = (1.0 - relaxation) * part + inv[:, here] * (mf[:, here] + total)

    fields = (u_a, u_b)
    for step in range(PRE_SWEEPS):
        sweep(fields[step % 2], fields[(step + 1) % 2])
        field = fields[(step + 1) % 2]
        window = windows[step]
        pack(field, window, own_slot)
        send_all(window, face_send.at[step], face_recv.at[step], 1)
        wait_all(window, face_send.at[step], face_recv.at[step], 1)
        gather(window)

    left = jnp.zeros((blocks, FACE), jnp.float32)
    added = jnp.zeros((blocks, FACE), jnp.float32)
    for x in range(SIDE):
        here = slice(x * FACE, (x + 1) * FACE)
        part, total = beside(field, x)
        driven = mf[:, here] + total
        coefficient = mc[:, here]
        left = left + (driven - (6.0 + coefficient) * part)
        added = added + coefficient
        base[:, here] = (1.0 - relaxation) * part + inv[:, here] * driven
    size = SIDE * FACE
    block_residual = jnp.sum(left, axis=1, keepdims=True) / size
    block_diag = 6.0 + jnp.sum(added, axis=1, keepdims=True) / size

    narrow = lax.broadcasted_iota(jnp.int32, (blocks, LANES), 1)
    links = jnp.zeros((blocks, LANES), jnp.int32)
    for b in range(blocks):
        for d in range(FACES):
            links = jnp.where((row == b) & (narrow == d), link_ref[b, d], links)
    message = links.astype(jnp.float32)
    message = jnp.where(narrow == FACES, block_residual, message)
    message = jnp.where(narrow == FACES + 1, block_diag, message)
    coarse[reach * nsub + sub] = message
    send_all(coarse, coarse_send, coarse_recv, reach)
    wait_all(coarse, coarse_send, coarse_recv, reach)

    shown = coarse[...]
    devices = shown.shape[0]
    shape = (devices, blocks, LANES)
    far = lax.broadcasted_iota(jnp.int32, shape, 2)
    index = lax.broadcasted_iota(jnp.int32, shape, 0) * blocks + lax.broadcasted_iota(
        jnp.int32, shape, 1
    )
    origin = ((pos - reach) * group).astype(jnp.float32)
    far_block = far.astype(jnp.float32) + origin
    linked = jnp.zeros(shape, jnp.float32)
    for d in range(FACES):
        link = shown[:, :, d : d + 1]
        linked = linked + ((link == far_block) & (link >= 0.0)).astype(jnp.float32)
    residuals = shown[:, :, FACES : FACES + 1]
    diags = shown[:, :, FACES + 1 : FACES + 2]
    diags = jnp.where(diags > 0.0, diags, 1.0)

    def turned(values):
        spread = jnp.where(index == far, values, 0.0)
        return jnp.sum(jnp.sum(spread, axis=0), axis=0, keepdims=True)

    errors = relaxation * residuals / diags
    for step in range(1, COARSE_SWEEPS):
        around = jnp.sum(linked * turned(errors)[None], axis=2, keepdims=True)
        errors = errors + relaxation * (residuals - diags * errors + around) / diags
    known = turned(errors)

    narrow_block = narrow.astype(jnp.float32) + origin
    own_row = (reach * nsub + sub) * blocks + row
    own_error = jnp.sum(jnp.where(narrow == own_row, known, 0.0), axis=1, keepdims=True)
    jumps = []
    for d in range(FACES):
        link = message[:, d : d + 1]
        hit = (link == narrow_block) & (link >= 0.0)
        jumps.append(jnp.sum(jnp.where(hit, known, 0.0), axis=1, keepdims=True) - own_error)
    plane = jnp.zeros((blocks, FACE), jnp.float32) + 6.0 * own_error
    plane = plane + jnp.where(strip == 0, jumps[2], 0.0)
    plane = plane + jnp.where(strip == SIDE - 1, jumps[3], 0.0)
    plane = plane + jnp.where(within == 0, jumps[4], 0.0)
    plane = plane + jnp.where(within == SIDE - 1, jumps[5], 0.0)
    kept = (1.0 - relaxation) * own_error
    for x in range(SIDE):
        here = slice(x * FACE, (x + 1) * FACE)
        extra = plane
        if x == 0:
            extra = extra + jumps[0]
        if x == SIDE - 1:
            extra = extra + jumps[1]
        out_ref[:, here] = base[:, here] + kept + inv[:, here] * extra

    for _, _, _, copy in peers:
        copy.wait_send()
    wait_sends(raw, raw_send, raw_recv, 1)
    for step in range(PRE_SWEEPS):
        wait_sends(windows[step], face_send.at[step], face_recv.at[step], 1)
    wait_sends(coarse, coarse_send, coarse_recv, reach)


def on_device(pressure, source_term, coefficient, new_slot, face_links):
    blocks, size = pressure.shape
    count = lax.axis_size("curve")
    nsub = lax.axis_size("sub")
    near = 3 * nsub
    wide = (2 * COARSE_SWEEPS + 1) * nsub
    others = max(1, nsub - 1)
    field = pltpu.VMEM((blocks, size), jnp.float32)
    landing = pltpu.VMEM((others, blocks, size), jnp.float32)
    dma = pltpu.SemaphoreType.DMA
    vmem = pl.BlockSpec(memory_space=pltpu.VMEM)
    smem = pl.BlockSpec(memory_space=pltpu.SMEM)
    return pl.pallas_call(
        functools.partial(kernel, count, nsub, blocks),
        out_shape=jax.ShapeDtypeStruct((blocks, size), jnp.float32),
        in_specs=[smem, smem, vmem, vmem, vmem],
        out_specs=vmem,
        scratch_shapes=[
            pltpu.VMEM((near, blocks, FACES * FACE + LANES), jnp.float32),
            pltpu.VMEM((near + 1, blocks, FACES * FACE), jnp.float32),
            pltpu.VMEM((near + 1, blocks, FACES * FACE), jnp.float32),
            pltpu.VMEM((near + 1, blocks, FACES * FACE), jnp.float32),
            pltpu.VMEM((FACES, blocks, FACE), jnp.float32),
            landing,
            landing,
            landing,
            field,
            field,
            field,
            field,
            field,
            field,
            pltpu.VMEM((wide, blocks, LANES), jnp.float32),
            dma((near,)),
            dma((near,)),
            dma((PRE_SWEEPS, near)),
            dma((PRE_SWEEPS, near)),
            dma((3, others)),
            dma((3, others)),
            dma((wide,)),
            dma((wide,)),
        ],
        compiler_params=pltpu.CompilerParams(
            collective_id=0, has_side_effects=True, vmem_limit_bytes=32 * 1024 * 1024
        ),
    )(new_slot, face_links, pressure, source_term, coefficient)


def solution(mesh):
    placed = (
        P(("curve", "sub"), None),
        P(("curve", "sub"), None),
        P(("curve", "sub"), None),
        P(("curve", "sub")),
        P(("curve", "sub"), None),
    )
    return jax.shard_map(
        on_device, mesh=mesh, in_specs=placed, out_specs=P(("curve", "sub"), None), check_vma=False
    )
```

time: 140 us -> 28.5 us (0.20)
  starting transfers between devices: 46.7 us -> 0 us
  local copies, waits for them, and re-layouts: 40.4 us -> 4.48 us
  Pallas kernels: 0 us -> 23.7 us
  waiting for transfers between devices: 17.7 us -> 0 us
  blocking collectives: 16.7 us -> 0 us
  other arithmetic: 13.2 us -> 0 us
  matrix products: 3.45 us -> 0 us
  between operations: 1.46 us -> 0.01 us
    ppermute x14 -> x0, starting transfers between devices: 43.2 us -> none  [the longest x7 34 us: with_halo(): lax.ppermute(lax.slice_in_dim(block, block.shape[dim] - width, None, axis...]
    pallas_call x0 -> x1, Pallas kernels: none -> 23.7 us  [on_device(): pl.pallas_call(functools.partial(kernel, count, nsub, blocks), out_shape=...]
    ppermute x14 -> x0, waiting for transfers between devices: 17.7 us -> none  [the longest x7 17.6 us: with_halo(): lax.ppermute(lax.slice_in_dim(block, 0, width, axis=dim), axis, backward)]
    slice x46 -> x0, local copies, waits for them, and re-layouts: 17.3 us -> none  [the longest x8 3.1 us: apply_operator(): x_plus = jnp.concatenate([cubes[:, 1:], sides[:, 1][:, None]], axis=1)]
    add x7 -> x0, other arithmetic: 10.1 us -> none  [the longest x3 6.04 us: sweep(): return field + relaxation * (source - image) / (6.0 + coefficient)]
    unnamed x4 -> x0, blocking collectives: 9.29 us -> none
    another operation x44 -> x0, local copies, waits for them, and re-layouts: 9.17 us -> none  [the longest x4 3.89 us: apply_operator(): sides[:, 2][:, :, None]]
    all_gather x4 -> x0, blocking collectives: 7.42 us -> none  [ghost_layers(): ranged = lax.all_gather(faces, 'sub', axis=0, tiled=True)]
  transfers between devices with their start and end apart: 15 -> 0, of which waited for: 6 -> 0; matrix products, arithmetic and copies ran while one was open for 11% -> 0% of each run, Pallas kernels for 0% -> 0%
where the time goes in v1:
time: 28.5 us; the launch traced here: 28.2 us
  Pallas kernels  23.7 us (83%)
  local copies, waits for them, and re-layouts  4.48 us (16%)
    pallas_call x1, Pallas kernels, on_device(): pl.pallas_call(functools.partial(kernel, count, nsub, blocks), out_shape=...  23.7 us
    unnamed x11, local copies, waits for them, and re-layouts  4.48 us

profile of v1, /device:TPU:0, one launch (start us, length us, event | category | flops | bytes accessed | tf_op | source)
XLA Modules:
  0.0 28.2 jit_solution(10828045209990662858)
XLA Ops:
  0.0 0.0 copy-start
  0.0 0.8 %copy-done = f32[4,4096]{1,0:T(4,128)S(1)} copy-done((f32[4,4096]{1,0:T(4,128)S(1)}, f32[4,4096]{1,0:T(4,128)}, u32[]{:S(2)}) %copy-start) | copy-done | bytes 65560
  0.8 0.0 copy-start.1
  0.8 0.8 %copy-done.1 = f32[4,4096]{1,0:T(4,128)S(1)} copy-done((f32[4,4096]{1,0:T(4,128)S(1)}, f32[4,4096]{1,0:T(4,128)}, u32[]{:S(2)}) %copy-start.1) | copy-done | bytes 65560
  1.7 0.0 copy-start.2
  1.7 0.8 %copy-done.2 = f32[4,4096]{1,0:T(4,128)S(1)} copy-done((f32[4,4096]{1,0:T(4,128)S(1)}, f32[4,4096]{1,0:T(4,128)}, u32[]{:S(2)}) %copy-start.2) | copy-done | bytes 65560
  2.5 0.0 copy-start.3
  2.5 0.7 %copy-done.3 = s32[4,6]{1,0:T(4,128)S(1)} copy-done((s32[4,6]{1,0:T(4,128)S(1)}, s32[4,6]{1,0:T(4,128)}, u32[]{:S(2)}) %copy-start.3) | copy-done | bytes 120
  3.2 0.0 copy-start.4
  3.2 0.7 %copy-done.4 = s32[4]{0:T(128)S(1)} copy-done((s32[4]{0:T(128)S(1)}, s32[4]{0:T(128)}, u32[]{:S(2)}) %copy-start.4) | copy-done | bytes 40
  3.9 23.7 %shard_map.55 = f32[4,4096]{1,0:T(4,128)S(1)} custom-call(s32[4]{0:T(128)S(1)} %copy-done.4, s32[4,6]{1,0:T(4,128)S(1)} %copy-done.3, f32[4,4096]{1,0:T(4,128)S(1)} %copy-done, f32[4,4096]{1,0:T(4,128)S(1)} %copy-done.1, f32[4,4096]{1,0:T(4,128)S(1)} %copy-done.2), custom_call_target="tpu_custom_call" | custom-call | tf_op jit(solution)/shard_map/pallas_call | solution.py:416
  27.6 0.6 %copy.7 = f32[4,4096]{1,0:T(4,128)} copy(f32[4,4096]{1,0:T(4,128)S(1)} %shard_map.55) | data formatting | bytes 131072
Async XLA Ops:
  0.0 0.8 %copy-start = (f32[4,4096]{1,0:T(4,128)S(1)}, f32[4,4096]{1,0:T(4,128)}, u32[]{:S(2)}) copy-start(f32[4,4096]{1,0:T(4,128)} %p_ref.1) | copy-start | bytes 196612
  0.8 0.8 %copy-start.1 = (f32[4,4096]{1,0:T(4,128)S(1)}, f32[4,4096]{1,0:T(4,128)}, u32[]{:S(2)}) copy-start(f32[4,4096]{1,0:T(4,128)} %f_ref.1) | copy-start | bytes 196612
  1.7 0.8 %copy-start.2 = (f32[4,4096]{1,0:T(4,128)S(1)}, f32[4,4096]{1,0:T(4,128)}, u32[]{:S(2)}) copy-start(f32[4,4096]{1,0:T(4,128)} %c_ref.1) | copy-start | bytes 196612
  2.5 0.7 %copy-start.3 = (s32[4,6]{1,0:T(4,128)S(1)}, s32[4,6]{1,0:T(4,128)}, u32[]{:S(2)}) copy-start(s32[4,6]{1,0:T(4,128)} %link_ref.1) | copy-start | bytes 292
  3.2 0.7 %copy-start.4 = (s32[4]{0:T(128)S(1)}, s32[4]{0:T(128)}, u32[]{:S(2)}) copy-start(s32[4]{0:T(128)} %slot_ref.1) | copy-start | bytes 52

commit v2 on v0

v2 whole, which is shorter than its diff:
```python
import functools

import jax
import jax.numpy as jnp
from jax import lax
from jax.experimental import pallas as pl
from jax.experimental.pallas import tpu as pltpu
from jax.sharding import PartitionSpec as P

PRE_SWEEPS = 2
COARSE_SWEEPS = 4
SIDE = 16
FACE = SIDE * SIDE
FACES = 6
LANES = 128
FLIP = (1, 0, 3, 2, 5, 4)

relaxation = 0.8
MESH = pl.DeviceIdType.MESH


def kernel(
    count,
    nsub,
    blocks,
    slot_hbm,
    link_hbm,
    p_hbm,
    f_hbm,
    c_hbm,
    out_ref,
    slot_ref,
    link_ref,
    stage_p,
    stage_f,
    stage_c,
    raw,
    first,
    window_a,
    window_b,
    ghosts,
    mf,
    mc,
    inv,
    field,
    base,
    coarse,
    local_sem,
    raw_send,
    raw_recv,
    face_send,
    face_recv,
    peer_send,
    peer_recv,
    coarse_send,
    coarse_recv,
):
    pos = lax.axis_index("curve")
    sub = lax.axis_index("sub")
    group = nsub * blocks
    reach = COARSE_SWEEPS
    wall = 3 * group
    near = (-1, 1)
    far = [t for t in range(-reach, reach + 1) if t]

    def exists(t):
        return (pos + t >= 0) & (pos + t < count)

    def guarded(t, action):
        if t == 0:
            action()
        else:
            pl.when(exists(t))(action)

    inputs = (
        (p_hbm, stage_p),
        (f_hbm, stage_f),
        (c_hbm, stage_c),
        (link_hbm, link_ref),
    )
    own_copies = [
        pltpu.make_async_copy(source, stage.at[sub], local_sem.at[k])
        for k, (source, stage) in enumerate(inputs)
    ]
    own_slots = pltpu.make_async_copy(slot_hbm, slot_ref, local_sem.at[len(inputs)])
    own_copies[0].start()
    own_slots.start()
    for copy in own_copies[1:]:
        copy.start()

    def clear(window, rows):
        window[rows] = jnp.zeros((rows.stop - rows.start,) + window.shape[1:], jnp.float32)

    for window in (first, window_a, window_b):
        clear(window, slice(wall, wall + 8))
    for t in near:

        @pl.when(jnp.logical_not(exists(t)))
        def _(t=t):
            for window in (window_a, window_b):
                clear(window, slice((t + 1) * group, (t + 2) * group))
            clear(raw, slice((t + 1) * nsub, (t + 2) * nsub))

    for t in far:

        @pl.when(jnp.logical_not(exists(t)))
        def _(t=t):
            clear(coarse, slice(t + reach, t + reach + 1))

    barrier = pltpu.get_barrier_semaphore()
    expected = 0
    for t in range(-reach, reach + 1):
        for ds in range(nsub if abs(t) <= 1 else 1):
            if t or ds:

                def greet(t=t, ds=ds):
                    pl.semaphore_signal(
                        barrier,
                        inc=1,
                        device_id=(pos + t, lax.rem(sub + ds, nsub)),
                        device_id_type=MESH,
                    )

                guarded(t, greet)
                expected = expected + (exists(t).astype(jnp.int32) if t else 1)
    pl.semaphore_wait(barrier, expected)

    def peer_copy(ds, k):
        source, stage = inputs[k]
        return pltpu.make_async_remote_copy(
            src_ref=source,
            dst_ref=stage.at[sub],
            send_sem=peer_send.at[k, ds - 1],
            recv_sem=peer_recv.at[k, nsub - ds - 1],
            device_id=(pos, lax.rem(sub + ds, nsub)),
            device_id_type=MESH,
        )

    def peer_landing(ds, k):
        source, stage = inputs[k]
        there = lax.rem(sub + ds, nsub)
        return pltpu.make_async_remote_copy(
            src_ref=source,
            dst_ref=stage.at[there],
            send_sem=peer_send.at[k, ds - 1],
            recv_sem=peer_recv.at[k, ds - 1],
            device_id=(pos, there),
            device_id_type=MESH,
        )

    for k in range(len(inputs)):
        for ds in range(1, nsub):
            peer_copy(ds, k).start()

    lane = lax.broadcasted_iota(jnp.int32, (blocks, LANES), 1)
    row = lax.broadcasted_iota(jnp.int32, (blocks, LANES), 0)
    group_lane = lax.broadcasted_iota(jnp.int32, (group, LANES), 1)
    group_row = lax.broadcasted_iota(jnp.int32, (group, LANES), 0)
    half = SIDE // 2

    def pack(tile, rows, at, store):
        strip = at // SIDE
        within = at % SIDE
        zero = jnp.zeros((rows, LANES), jnp.float32)
        y_low = [zero, zero]
        y_high = [zero, zero]
        z_low = [zero, zero]
        z_high = [zero, zero]
        for x in range(SIDE):
            part = tile(x, 0), tile(x, 1)
            k, m = divmod(x, half)
            for h in range(2):
                if x == 0:
                    store(0, h, part[h])
                if x == SIDE - 1:
                    store(1, h, part[h])
                z_low[h] = jnp.where(within == x, pltpu.roll(part[h], x, 1), z_low[h])
                z_high[h] = jnp.where(
                    within == x, pltpu.roll(part[h], (x - SIDE + 1) % LANES, 1), z_high[h]
                )
            y_low[k] = jnp.where(strip == m, pltpu.roll(part[0], SIDE * m, 1), y_low[k])
            y_high[k] = jnp.where(
                strip == m, pltpu.roll(part[1], (SIDE * (m + 1)) % LANES, 1), y_high[k]
            )
        for d, packed in ((2, y_low), (3, y_high), (4, z_low), (5, z_high)):
            for h in range(2):
                store(d, h, packed[h])

    def spot(d, h):
        return slice(d * FACE + h * LANES, d * FACE + (h + 1) * LANES)

    def cells(x, h):
        return slice(x * FACE + h * LANES, x * FACE + (h + 1) * LANES)

    own_slot = nsub + sub
    own_copies[0].wait()

    def store_raw(d, h, value):
        raw[own_slot, :, spot(d, h)] = value

    pack(lambda x, h: stage_p[sub, :, cells(x, h)], blocks, lane, store_raw)
    own_slots.wait()
    slots = jnp.zeros((blocks, LANES), jnp.int32)
    for j in range(blocks):
        slots = jnp.where(row == j, slot_ref[j], slots)
    raw[own_slot, :, FACES * FACE :] = slots.astype(jnp.float32)

    def raw_copy(t, ds):
        there = lax.rem(sub + ds, nsub)
        return pltpu.make_async_remote_copy(
            src_ref=raw.at[own_slot],
            dst_ref=raw.at[(1 - t) * nsub + sub],
            send_sem=raw_send.at[(1 + t) * nsub + there],
            recv_sem=raw_recv.at[(1 - t) * nsub + sub],
            device_id=(pos + t, there),
            device_id_type=MESH,
        )

    def raw_landing(t, ds):
        there = lax.rem(sub + ds, nsub)
        slot = (1 + t) * nsub + there
        return pltpu.make_async_remote_copy(
            src_ref=raw.at[own_slot],
            dst_ref=raw.at[slot],
            send_sem=raw_send.at[slot],
            recv_sem=raw_recv.at[slot],
            device_id=(pos + t, there),
            device_id_type=MESH,
        )

    raw_partners = [(t, ds) for t in (-1, 1, 0) for ds in range(nsub) if t or ds]
    for t, ds in raw_partners:
        guarded(t, lambda t=t, ds=ds: raw_copy(t, ds).start())

    for copy in own_copies[1:]:
        copy.wait()
    for t, ds in raw_partners:
        if t == 0:
            raw_landing(t, ds).wait_recv()
    order = group_row.astype(jnp.float32)

    def chosen(t):
        return [
            (s, j, raw[(1 + t) * nsub + s, j : j + 1, FACES * FACE :] == order)
            for s in range(nsub)
            for j in range(blocks)
        ]

    picks = chosen(0)
    for k, target in enumerate((field, mf, mc)):
        stage = inputs[k][1]
        for ds in range(1, nsub):
            peer_landing(ds, k).wait_recv()
        for x in range(SIDE):
            for h in range(2):
                total = jnp.zeros((group, LANES), jnp.float32)
                for s, j, pick in picks:
                    total = jnp.where(pick, stage[s, j : j + 1, cells(x, h)], total)
                target[:, cells(x, h)] = total
    for ds in range(1, nsub):
        peer_landing(ds, len(inputs) - 1).wait_recv()

    start = (pos - 1) * group
    places = []
    for s in range(nsub):
        for b in range(blocks):
            for d in range(FACES):
                link = link_ref[s, b, d]
                place = jnp.where(link < 0, wall, jnp.clip(link - start, 0, wall - 1))
                places.append((s * blocks + b, d, place))

    def gather(window):
        for b, d, place in places:
            flipped = FLIP[d]
            ghosts[d, pl.ds(b, 1), :] = window[
                pl.ds(place, 1), flipped * FACE : (flipped + 1) * FACE
            ]

    strip = group_lane // SIDE
    within = group_lane % SIDE

    def interior(x, tile):
        part = tile(x, 0), tile(x, 1)
        up = [pltpu.roll(v, SIDE, 1) for v in part]
        down = [pltpu.roll(v, LANES - SIDE, 1) for v in part]
        found = []
        for h in range(2):
            total = jnp.where(within == 0, 0.0, pltpu.roll(part[h], 1, 1))
            total = total + jnp.where(within == SIDE - 1, 0.0, pltpu.roll(part[h], LANES - 1, 1))
            total = total + jnp.where(strip == 0, up[0] if h else 0.0, up[h])
            total = total + jnp.where(
                strip == half - 1, 0.0 if h else down[1], down[h]
            )
            if x > 0:
                total = total + tile(x - 1, h)
            if x < SIDE - 1:
                total = total + tile(x + 1, h)
            found.append(total)
        return part, found

    def outside(x, h):
        k, m = divmod(x, half)
        halves = slice(h * LANES, (h + 1) * LANES)
        total = jnp.where(within == 0, pltpu.roll(ghosts[4, :, halves], (-x) % LANES, 1), 0.0)
        total = jnp.where(
            within == SIDE - 1, pltpu.roll(ghosts[5, :, halves], SIDE - 1 - x, 1), total
        )
        source = slice(k * LANES, (k + 1) * LANES)
        if h == 0:
            side = pltpu.roll(ghosts[2, :, source], (-SIDE * m) % LANES, 1)
            total = total + jnp.where(strip == 0, side, 0.0)
        else:
            side = pltpu.roll(ghosts[3, :, source], SIDE * (half - 1 - m), 1)
            total = total + jnp.where(strip == half - 1, side, 0.0)
        if x == 0:
            total = total + ghosts[0, :, halves]
        if x == SIDE - 1:
            total = total + ghosts[1, :, halves]
        return total

    def value(x, h):
        return field[:, cells(x, h)]

    def prepare():
        for x in range(SIDE):
            part, found = interior(x, value)
            for h in range(2):
                here = cells(x, h)
                base[:, here] = (1.0 - relaxation) * part[h] + inv[:, here] * (
                    mf[:, here] + found[h]
                )

    for x in range(SIDE):
        for h in range(2):
            inv[:, cells(x, h)] = relaxation / (6.0 + mc[:, cells(x, h)])
    prepare()

    for t in (0, -1, 1):
        if t:
            for ds in range(nsub):
                guarded(t, lambda t=t, ds=ds: raw_landing(t, ds).wait_recv())
        picks = chosen(t)
        for d in range(FACES):
            for h in range(2):
                total = jnp.zeros((group, LANES), jnp.float32)
                for s, j, pick in picks:
                    total = jnp.where(
                        pick, raw[(1 + t) * nsub + s, j : j + 1, spot(d, h)], total
                    )
                first[(1 + t) * group : (2 + t) * group, spot(d, h)] = total
    gather(first)

    def face_copy(window, step, t):
        return pltpu.make_async_remote_copy(
            src_ref=window.at[pl.ds(group, group)],
            dst_ref=window.at[pl.ds((1 - t) * group, group)],
            send_sem=face_send.at[step, 1 + t],
            recv_sem=face_recv.at[step, 1 - t],
            device_id=(pos + t, sub),
            device_id_type=MESH,
        )

    def face_landing(window, step, t):
        return pltpu.make_async_remote_copy(
            src_ref=window.at[pl.ds(group, group)],
            dst_ref=window.at[pl.ds((1 + t) * group, group)],
            send_sem=face_send.at[step, 1 + t],
            recv_sem=face_recv.at[step, 1 + t],
            device_id=(pos + t, sub),
            device_id_type=MESH,
        )

    windows = (window_a, window_b)
    for step in range(PRE_SWEEPS):
        window = windows[step]

        def store_faces(d, h, packed):
            window[group : 2 * group, spot(d, h)] = packed

        def swept(x, h):
            here = cells(x, h)
            fresh = base[:, here] + inv[:, here] * outside(x, h)
            field[:, here] = fresh
            return fresh

        pack(swept, group, group_lane, store_faces)
        for t in near:
            guarded(t, lambda t=t: face_copy(window, step, t).start())
        prepare()
        for t in near:
            guarded(t, lambda t=t: face_landing(window, step, t).wait_recv())
        gather(window)

    left = jnp.zeros((group, LANES), jnp.float32)
    added = jnp.zeros((group, LANES), jnp.float32)
    for x in range(SIDE):
        for h in range(2):
            here = cells(x, h)
            fresh = base[:, here] + inv[:, here] * outside(x, h)
            diagonal = 6.0 + mc[:, here]
            left = left + (fresh - field[:, here]) * diagonal
            added = added + mc[:, here]
            base[:, here] = fresh
    size = SIDE * FACE
    block_residual = jnp.sum(left, axis=1, keepdims=True) / (size * relaxation)
    block_diag = 6.0 + jnp.sum(added, axis=1, keepdims=True) / size

    links = jnp.zeros((group, LANES), jnp.int32)
    for s in range(nsub):
        for b in range(blocks):
            for d in range(FACES):
                links = jnp.where(
                    (group_row == s * blocks + b) & (group_lane == d), link_ref[s, b, d], links
                )
    message = links.astype(jnp.float32)
    message = jnp.where(group_lane == FACES, block_residual, message)
    message = jnp.where(group_lane == FACES + 1, block_diag, message)
    coarse[reach] = message

    def coarse_copy(t):
        return pltpu.make_async_remote_copy(
            src_ref=coarse.at[reach],
            dst_ref=coarse.at[reach - t],
            send_sem=coarse_send.at[reach + t],
            recv_sem=coarse_recv.at[reach - t],
            device_id=(pos + t, sub),
            device_id_type=MESH,
        )

    def coarse_landing(t):
        return pltpu.make_async_remote_copy(
            src_ref=coarse.at[reach],
            dst_ref=coarse.at[reach + t],
            send_sem=coarse_send.at[reach + t],
            recv_sem=coarse_recv.at[reach + t],
            device_id=(pos + t, sub),
            device_id_type=MESH,
        )

    for t in far:
        guarded(t, lambda t=t: coarse_copy(t).start())
    for t in far:
        guarded(t, lambda t=t: coarse_landing(t).wait_recv())

    shown = coarse[...]
    shape = (2 * reach + 1, group, LANES)
    column = lax.broadcasted_iota(jnp.int32, shape, 2)
    index = lax.broadcasted_iota(jnp.int32, shape, 0) * group + lax.broadcasted_iota(
        jnp.int32, shape, 1
    )
    origin = ((pos - reach) * group).astype(jnp.float32)
    numbered = column.astype(jnp.float32) + origin
    linked = jnp.zeros(shape, jnp.float32)
    for d in range(FACES):
        link = shown[:, :, d : d + 1]
        linked = linked + ((link == numbered) & (link >= 0.0)).astype(jnp.float32)
    residuals = shown[:, :, FACES : FACES + 1]
    diags = shown[:, :, FACES + 1 : FACES + 2]
    diags = jnp.where(diags > 0.0, diags, 1.0)

    def turned(values):
        spread = jnp.where(index == column, values, 0.0)
        return jnp.sum(jnp.sum(spread, axis=0), axis=0, keepdims=True)

    scaled = relaxation / diags
    driven = scaled * residuals
    errors = driven
    for step in range(1, COARSE_SWEEPS):
        around = jnp.sum(linked * turned(errors)[None], axis=2, keepdims=True)
        errors = (1.0 - relaxation) * errors + driven + scaled * around
    known = turned(errors)

    own_numbered = group_lane.astype(jnp.float32) + origin
    own_error = jnp.sum(
        jnp.where(group_lane == reach * group + group_row, known, 0.0), axis=1, keepdims=True
    )
    jumps = []
    for d in range(FACES):
        link = message[:, d : d + 1]
        hit = (link == own_numbered) & (link >= 0.0)
        jumps.append(jnp.sum(jnp.where(hit, known, 0.0), axis=1, keepdims=True) - own_error)
    plane = jnp.zeros((group, LANES), jnp.float32) + 6.0 * own_error
    plane = plane + jnp.where(within == 0, jumps[4], 0.0)
    plane = plane + jnp.where(within == SIDE - 1, jumps[5], 0.0)
    planes = (
        plane + jnp.where(strip == 0, jumps[2], 0.0),
        plane + jnp.where(strip == half - 1, jumps[3], 0.0),
    )
    kept = (1.0 - relaxation) * own_error + jnp.zeros((group, LANES), jnp.float32)
    for x in range(SIDE):
        for h in range(2):
            here = cells(x, h)
            extra = planes[h]
            if x == 0:
                extra = extra + jumps[0]
            if x == SIDE - 1:
                extra = extra + jumps[1]
            whole = base[:, here] + kept + inv[:, here] * extra
            result = whole[:blocks]
            for s in range(1, nsub):
                result = jnp.where(sub == s, whole[s * blocks : (s + 1) * blocks], result)
            out_ref[:, here] = result

    for k in range(len(inputs)):
        for ds in range(1, nsub):
            peer_copy(ds, k).wait_send()
    for t, ds in raw_partners:
        guarded(t, lambda t=t, ds=ds: raw_copy(t, ds).wait_send())
    for step in range(PRE_SWEEPS):
        for t in near:
            guarded(t, lambda t=t: face_copy(windows[step], step, t).wait_send())
    for t in far:
        guarded(t, lambda t=t: coarse_copy(t).wait_send())


def on_device(pressure, source_term, coefficient, new_slot, face_links):
    blocks, size = pressure.shape
    count = lax.axis_size("curve")
    nsub = lax.axis_size("sub")
    group = nsub * blocks
    others = max(1, nsub - 1)
    stage = pltpu.VMEM((nsub, blocks, size), jnp.float32)
    field = pltpu.VMEM((group, size), jnp.float32)
    window = pltpu.VMEM((3 * group + 8, FACES * FACE), jnp.float32)
    dma = pltpu.SemaphoreType.DMA
    hbm = pl.BlockSpec(memory_space=pltpu.HBM)
    return pl.pallas_call(
        functools.partial(kernel, count, nsub, blocks),
        out_shape=jax.ShapeDtypeStruct((blocks, size), jnp.float32),
        in_specs=[hbm] * 5,
        out_specs=pl.BlockSpec(memory_space=pltpu.VMEM),
        scratch_shapes=[
            pltpu.SMEM((blocks,), jnp.int32),
            pltpu.SMEM((nsub, blocks, FACES), jnp.int32),
            stage,
            stage,
            stage,
            pltpu.VMEM((3 * nsub, blocks, FACES * FACE + LANES), jnp.float32),
            window,
            window,
            window,
            pltpu.VMEM((FACES, group, FACE), jnp.float32),
            field,
            field,
            field,
            field,
            field,
            pltpu.VMEM((2 * COARSE_SWEEPS + 1, group, LANES), jnp.float32),
            dma((5,)),
            dma((3 * nsub,)),
            dma((3 * nsub,)),
            dma((PRE_SWEEPS, 3)),
            dma((PRE_SWEEPS, 3)),
            dma((4, others)),
            dma((4, others)),
            dma((2 * COARSE_SWEEPS + 1,)),
            dma((2 * COARSE_SWEEPS + 1,)),
        ],
        compiler_params=pltpu.CompilerParams(
            collective_id=0, has_side_effects=True, vmem_limit_bytes=63 * 1024 * 1024
        ),
    )(new_slot, face_links, pressure, source_term, coefficient)


def solution(mesh):
    placed = (
        P(("curve", "sub"), None),
        P(("curve", "sub"), None),
        P(("curve", "sub"), None),
        P(("curve", "sub")),
        P(("curve", "sub"), None),
    )
    return jax.shard_map(
        on_device, mesh=mesh, in_specs=placed, out_specs=P(("curve", "sub"), None), check_vma=False
    )
```

time: 140 us -> 25.4 us (0.18)
  starting transfers between devices: 46.7 us -> 0 us
  local copies, waits for them, and re-layouts: 40.4 us -> 1.47 us
  Pallas kernels: 0 us -> 23.7 us
  waiting for transfers between devices: 17.7 us -> 0 us
  blocking collectives: 16.7 us -> 0 us
  other arithmetic: 13.2 us -> 0 us
  matrix products: 3.45 us -> 0 us
  between operations: 1.46 us -> 0.01 us
    ppermute x14 -> x0, starting transfers between devices: 43.2 us -> none  [the longest x7 34 us: with_halo(): lax.ppermute(lax.slice_in_dim(block, block.shape[dim] - width, None, axis...]
    pallas_call x0 -> x1, Pallas kernels: none -> 23.7 us  [on_device(): pl.pallas_call(functools.partial(kernel, count, nsub, blocks), out_shape=...]
    ppermute x14 -> x0, waiting for transfers between devices: 17.7 us -> none  [the longest x7 17.6 us: with_halo(): lax.ppermute(lax.slice_in_dim(block, 0, width, axis=dim), axis, backward)]
    slice x46 -> x0, local copies, waits for them, and re-layouts: 17.3 us -> none  [the longest x8 3.1 us: apply_operator(): x_plus = jnp.concatenate([cubes[:, 1:], sides[:, 1][:, None]], axis=1)]
    add x7 -> x0, other arithmetic: 10.1 us -> none  [the longest x3 6.04 us: sweep(): return field + relaxation * (source - image) / (6.0 + coefficient)]
    unnamed x4 -> x0, blocking collectives: 9.29 us -> none
    another operation x44 -> x0, local copies, waits for them, and re-layouts: 9.17 us -> none  [the longest x4 3.89 us: apply_operator(): sides[:, 2][:, :, None]]
    all_gather x4 -> x0, blocking collectives: 7.42 us -> none  [ghost_layers(): ranged = lax.all_gather(faces, 'sub', axis=0, tiled=True)]
  transfers between devices with their start and end apart: 15 -> 0, of which waited for: 6 -> 0; matrix products, arithmetic and copies ran while one was open for 11% -> 0% of each run, Pallas kernels for 0% -> 0%
where the time goes in v2:
time: 25.4 us; the launch traced here: 25.2 us
  Pallas kernels  23.7 us (93%)
  local copies, waits for them, and re-layouts  1.47 us (6%)
    pallas_call x1, Pallas kernels, on_device(): pl.pallas_call(functools.partial(kernel, count, nsub, blocks), out_shape=...  23.7 us
    unnamed x1, local copies, waits for them, and re-layouts  1.47 us

profile of v2, /device:TPU:0, one launch (start us, length us, event | category | flops | bytes accessed | tf_op | source)
XLA Modules:
  0.0 25.2 jit_solution(6461565061934757308)
XLA Ops:
  0.0 23.7 %shard_map.55 = f32[4,4096]{1,0:T(4,128)} custom-call(s32[4]{0:T(128)} %slot_hbm.1, s32[4,6]{1,0:T(4,128)} %link_hbm.1, f32[4,4096]{1,0:T(4,128)} %p_hbm.1, f32[4,4096]{1,0:T(4,128)} %f_hbm.1, f32[4,4096]{1,0:T(4,128)} %c_hbm.1), custom_call_target="tpu_custom_call" | custom-call | tf_op jit(solution)/shard_map/pallas_call | solution.py:527
  23.7 1.5 %copy.7 = f32[4,4096]{1,0:T(4,128)} copy(f32[4,4096]{1,0:T(4,128)} %shard_map.55) | data formatting | bytes 131072

commit v3 on v2

--- a/solution.py
+++ b/solution.py
@@ -10,6 +10,7 @@
 PRE_SWEEPS = 2
 COARSE_SWEEPS = 4
 SIDE = 16
+GREETED = 3
 FACE = SIDE * SIDE
 FACES = 6
 LANES = 128
@@ -58,7 +59,8 @@
     pos = lax.axis_index("curve")
     sub = lax.axis_index("sub")
     group = nsub * blocks
-    reach = COARSE_SWEEPS
+    reach = COARSE_SWEEPS + 1
+    greeted = GREETED
     wall = 3 * group
     near = (-1, 1)
     far = [t for t in range(-reach, reach + 1) if t]
@@ -71,6 +73,23 @@
             action()
         else:
             pl.when(exists(t))(action)
+
+    barrier = pltpu.get_barrier_semaphore()
+    expected = 0
+    for t in sorted(range(-greeted, greeted + 1), key=abs):
+        for ds in range(nsub if abs(t) <= 1 else 1):
+            if t or ds:
+
+                def greet(t=t, ds=ds):
+                    pl.semaphore_signal(
+                        barrier,
+                        inc=1,
+                        device_id=(pos + t, lax.rem(sub + ds, nsub)),
+                        device_id_type=MESH,
+                    )
+
+                guarded(t, greet)
+                expected = expected + (exists(t).astype(jnp.int32) if t else 1)
 
     inputs = (
         (p_hbm, stage_p),
@@ -107,24 +126,6 @@
         def _(t=t):
             clear(coarse, slice(t + reach, t + reach + 1))
 
-    barrier = pltpu.get_barrier_semaphore()
-    expected = 0
-    for t in range(-reach, reach + 1):
-        for ds in range(nsub if abs(t) <= 1 else 1):
-            if t or ds:
-
-                def greet(t=t, ds=ds):
-                    pl.semaphore_signal(
-                        barrier,
-                        inc=1,
-                        device_id=(pos + t, lax.rem(sub + ds, nsub)),
-                        device_id_type=MESH,
-                    )
-
-                guarded(t, greet)
-                expected = expected + (exists(t).astype(jnp.int32) if t else 1)
-    pl.semaphore_wait(barrier, expected)
-
     def peer_copy(ds, k):
         source, stage = inputs[k]
         return pltpu.make_async_remote_copy(
@@ -147,10 +148,6 @@
             device_id=(pos, there),
             device_id_type=MESH,
         )
-
-    for k in range(len(inputs)):
-        for ds in range(1, nsub):
-            peer_copy(ds, k).start()
 
     lane = lax.broadcasted_iota(jnp.int32, (blocks, LANES), 1)
     row = lax.broadcasted_iota(jnp.int32, (blocks, LANES), 0)
@@ -229,8 +226,12 @@
         )
 
     raw_partners = [(t, ds) for t in (-1, 1, 0) for ds in range(nsub) if t or ds]
+    pl.semaphore_wait(barrier, expected)
     for t, ds in raw_partners:
         guarded(t, lambda t=t, ds=ds: raw_copy(t, ds).start())
+    for k in range(len(inputs)):
+        for ds in range(1, nsub):
+            peer_copy(ds, k).start()
 
     for copy in own_copies[1:]:
         copy.wait()
@@ -335,6 +336,22 @@
             inv[:, cells(x, h)] = relaxation / (6.0 + mc[:, cells(x, h)])
     prepare()
 
+    size = SIDE * FACE
+    links = jnp.zeros((group, LANES), jnp.int32)
+    for s in range(nsub):
+        for b in range(blocks):
+            for d in range(FACES):
+                links = jnp.where(
+                    (group_row == s * blocks + b) & (group_lane == d), link_ref[s, b, d], links
+                )
+    links = links.astype(jnp.float32)
+    added = jnp.zeros((group, LANES), jnp.float32)
+    for x in range(SIDE):
+        for h in range(2):
+            added = added + mc[:, cells(x, h)]
+    block_diag = 6.0 + jnp.sum(added, axis=1, keepdims=True) / size
+    message = jnp.where(group_lane == FACES + 1, block_diag, links)
+
     for t in (0, -1, 1):
         if t:
             for ds in range(nsub):
@@ -370,6 +387,48 @@
             device_id_type=MESH,
         )
 
+    def coarse_copy(t):
+        return pltpu.make_async_remote_copy(
+            src_ref=coarse.at[reach],
+            dst_ref=coarse.at[reach - t],
+            send_sem=coarse_send.at[reach + t],
+            recv_sem=coarse_recv.at[reach - t],
+            device_id=(pos + t, sub),
+            device_id_type=MESH,
+        )
+
+    def coarse_landing(t):
+        return pltpu.make_async_remote_copy(
+            src_ref=coarse.at[reach],
+            dst_ref=coarse.at[reach + t],
+            send_sem=coarse_send.at[reach + t],
+            recv_sem=coarse_recv.at[reach + t],
+            device_id=(pos + t, sub),
+            device_id_type=MESH,
+        )
+
+    def send_coarse(window):
+        own = slice(group, 2 * group)
+        left = jnp.zeros((group, LANES), jnp.float32)
+        for x in range(SIDE):
+            for h in range(2):
+                here = cells(x, h)
+                left = left + (mf[:, here] - mc[:, here] * field[:, here])
+        block = group_lane % group == group_row
+        lanes_row = lax.broadcasted_iota(jnp.int32, (8, LANES), 0)
+        sums = jnp.zeros((8, LANES), jnp.float32)
+        for d in range(FACES):
+            both = window[own, spot(d, 0)] + window[own, spot(d, 1)]
+            left = left - both
+            total = jnp.sum(both, axis=1, keepdims=True) / size
+            line = jnp.sum(jnp.where(block, total, 0.0), axis=0, keepdims=True)
+            sums = jnp.where(lanes_row == d, line, sums)
+        own_part = jnp.sum(left, axis=1, keepdims=True) / size
+        coarse[reach, 0:group, :] = jnp.where(group_lane == FACES, own_part, message)
+        coarse[reach, group : group + 8, :] = sums
+        for t in sorted(far, key=lambda t: -abs(t)):
+            guarded(t, lambda t=t: coarse_copy(t).start())
+
     windows = (window_a, window_b)
     for step in range(PRE_SWEEPS):
         window = windows[step]
@@ -384,65 +443,21 @@
             return fresh
 
         pack(swept, group, group_lane, store_faces)
+        if step == PRE_SWEEPS - 1:
+            send_coarse(window)
         for t in near:
             guarded(t, lambda t=t: face_copy(window, step, t).start())
         prepare()
+        if step == PRE_SWEEPS - 1:
+            break
         for t in near:
             guarded(t, lambda t=t: face_landing(window, step, t).wait_recv())
         gather(window)
 
-    left = jnp.zeros((group, LANES), jnp.float32)
-    added = jnp.zeros((group, LANES), jnp.float32)
-    for x in range(SIDE):
-        for h in range(2):
-            here = cells(x, h)
-            fresh = base[:, here] + inv[:, here] * outside(x, h)
-            diagonal = 6.0 + mc[:, here]
-            left = left + (fresh - field[:, here]) * diagonal
-            added = added + mc[:, here]
-            base[:, here] = fresh
-    size = SIDE * FACE
-    block_residual = jnp.sum(left, axis=1, keepdims=True) / (size * relaxation)
-    block_diag = 6.0 + jnp.sum(added, axis=1, keepdims=True) / size
-
-    links = jnp.zeros((group, LANES), jnp.int32)
-    for s in range(nsub):
-        for b in range(blocks):
-            for d in range(FACES):
-                links = jnp.where(
-                    (group_row == s * blocks + b) & (group_lane == d), link_ref[s, b, d], links
-                )
-    message = links.astype(jnp.float32)
-    message = jnp.where(group_lane == FACES, block_residual, message)
-    message = jnp.where(group_lane == FACES + 1, block_diag, message)
-    coarse[reach] = message
-
-    def coarse_copy(t):
-        return pltpu.make_async_remote_copy(
-            src_ref=coarse.at[reach],
-            dst_ref=coarse.at[reach - t],
-            send_sem=coarse_send.at[reach + t],
-            recv_sem=coarse_recv.at[reach - t],
-            device_id=(pos + t, sub),
-            device_id_type=MESH,
-        )
-
-    def coarse_landing(t):
-        return pltpu.make_async_remote_copy(
-            src_ref=coarse.at[reach],
-            dst_ref=coarse.at[reach + t],
-            send_sem=coarse_send.at[reach + t],
-            recv_sem=coarse_recv.at[reach + t],
-            device_id=(pos + t, sub),
-            device_id_type=MESH,
-        )
-
-    for t in far:
-        guarded(t, lambda t=t: coarse_copy(t).start())
     for t in far:
         guarded(t, lambda t=t: coarse_landing(t).wait_recv())
 
-    shown = coarse[...]
+    shown = coarse[:, 0:group, :]
     shape = (2 * reach + 1, group, LANES)
     column = lax.broadcasted_iota(jnp.int32, shape, 2)
     index = lax.broadcasted_iota(jnp.int32, shape, 0) * group + lax.broadcasted_iota(
@@ -450,11 +465,19 @@
     )
     origin = ((pos - reach) * group).astype(jnp.float32)
     numbered = column.astype(jnp.float32) + origin
+    face_sums = jnp.zeros((8, LANES), jnp.float32)
+    narrow = lax.broadcasted_iota(jnp.int32, (8, LANES), 1)
+    for k in range(2 * reach + 1):
+        face_sums = jnp.where(narrow // group == k, coarse[k, group : group + 8, :], face_sums)
     linked = jnp.zeros(shape, jnp.float32)
+    entering = jnp.zeros(shape, jnp.float32)
     for d in range(FACES):
         link = shown[:, :, d : d + 1]
-        linked = linked + ((link == numbered) & (link >= 0.0)).astype(jnp.float32)
-    residuals = shown[:, :, FACES : FACES + 1]
+        hit = (link == numbered) & (link >= 0.0)
+        linked = linked + hit.astype(jnp.float32)
+        flipped = FLIP[d]
+        entering = entering + jnp.where(hit, face_sums[flipped : flipped + 1][None], 0.0)
+    residuals = shown[:, :, FACES : FACES + 1] + jnp.sum(entering, axis=2, keepdims=True)
     diags = shown[:, :, FACES + 1 : FACES + 2]
     diags = jnp.where(diags > 0.0, diags, 1.0)
 
@@ -487,10 +510,14 @@
         plane + jnp.where(strip == half - 1, jumps[3], 0.0),
     )
     kept = (1.0 - relaxation) * own_error + jnp.zeros((group, LANES), jnp.float32)
+    last = PRE_SWEEPS - 1
+    for t in near:
+        guarded(t, lambda t=t: face_landing(windows[last], last, t).wait_recv())
+    gather(windows[last])
     for x in range(SIDE):
         for h in range(2):
             here = cells(x, h)
-            extra = planes[h]
+            extra = planes[h] + outside(x, h)
             if x == 0:
                 extra = extra + jumps[0]
             if x == SIDE - 1:
@@ -545,7 +572,7 @@
             field,
             field,
             field,
-            pltpu.VMEM((2 * COARSE_SWEEPS + 1, group, LANES), jnp.float32),
+            pltpu.VMEM((2 * COARSE_SWEEPS + 3, group + 8, LANES), jnp.float32),
             dma((5,)),
             dma((3 * nsub,)),
             dma((3 * nsub,)),
@@ -553,8 +580,8 @@
             dma((PRE_SWEEPS, 3)),
             dma((4, others)),
             dma((4, others)),
-            dma((2 * COARSE_SWEEPS + 1,)),
-            dma((2 * COARSE_SWEEPS + 1,)),
+            dma((2 * COARSE_SWEEPS + 3,)),
+            dma((2 * COARSE_SWEEPS + 3,)),
         ],
         compiler_params=pltpu.CompilerParams(
             collective_id=0, has_side_effects=True, vmem_limit_bytes=63 * 1024 * 1024

time: 25.4 us -> 21.7 us (0.85)
  Pallas kernels: 23.7 us -> 20 us
    pallas_call x1, Pallas kernels: 23.7 us -> 20 us  [on_device(): pl.pallas_call(functools.partial(kernel, count, nsub, blocks), out_shape=...]
where the time goes in v3:
time: 21.7 us; the launch traced here: 21.5 us
  Pallas kernels  20 us (92%)
  local copies, waits for them, and re-layouts  1.47 us (7%)
    pallas_call x1, Pallas kernels, on_device(): pl.pallas_call(functools.partial(kernel, count, nsub, blocks), out_shape=...  20 us
    unnamed x1, local copies, waits for them, and re-layouts  1.47 us

profile of v3, /device:TPU:0, one launch (start us, length us, event | category | flops | bytes accessed | tf_op | source)
XLA Modules:
  0.0 21.5 jit_solution(11047795850044311588)
XLA Ops:
  0.0 20.0 %shard_map.55 = f32[4,4096]{1,0:T(4,128)} custom-call(s32[4]{0:T(128)} %slot_hbm.1, s32[4,6]{1,0:T(4,128)} %link_hbm.1, f32[4,4096]{1,0:T(4,128)} %p_hbm.1, f32[4,4096]{1,0:T(4,128)} %f_hbm.1, f32[4,4096]{1,0:T(4,128)} %c_hbm.1), custom_call_target="tpu_custom_call" | custom-call | tf_op jit(solution)/shard_map/pallas_call | solution.py:554
  20.0 1.5 %copy.7 = f32[4,4096]{1,0:T(4,128)} copy(f32[4,4096]{1,0:T(4,128)} %shard_map.55) | data formatting | bytes 131072

commit v4 on v3

--- a/solution.py
+++ b/solution.py
@@ -32,14 +32,18 @@
     out_ref,
     slot_ref,
     link_ref,
+    near_links,
     stage_p,
     stage_f,
     stage_c,
     raw,
     first,
-    window_a,
-    window_b,
+    window,
+    last_faces,
+    parts_out,
+    parts_in,
     ghosts,
+    own_ghosts,
     mf,
     mc,
     inv,
@@ -55,6 +59,8 @@
     peer_recv,
     coarse_send,
     coarse_recv,
+    link_send,
+    link_recv,
 ):
     pos = lax.axis_index("curve")
     sub = lax.axis_index("sub")
@@ -110,14 +116,15 @@
     def clear(window, rows):
         window[rows] = jnp.zeros((rows.stop - rows.start,) + window.shape[1:], jnp.float32)
 
-    for window in (first, window_a, window_b):
-        clear(window, slice(wall, wall + 8))
+    clear(first, slice(wall, wall + 8))
+    clear(window, slice(wall, wall + 8))
+    clear(last_faces, slice(group, group + 8))
     for t in near:
 
         @pl.when(jnp.logical_not(exists(t)))
         def _(t=t):
-            for window in (window_a, window_b):
-                clear(window, slice((t + 1) * group, (t + 2) * group))
+            clear(window, slice((t + 1) * group, (t + 2) * group))
+            clear(parts_in, slice((t + 1) // 2, (t + 1) // 2 + 1))
             clear(raw, slice((t + 1) * nsub, (t + 2) * nsub))
 
     for t in far:
@@ -233,6 +240,29 @@
         for ds in range(1, nsub):
             peer_copy(ds, k).start()
 
+    def link_copy(t):
+        return pltpu.make_async_remote_copy(
+            src_ref=link_hbm,
+            dst_ref=near_links.at[(1 - t) // 2],
+            send_sem=link_send.at[(1 + t) // 2],
+            recv_sem=link_recv.at[(1 - t) // 2],
+            device_id=(pos + t, sub),
+            device_id_type=MESH,
+        )
+
+    def link_landing(t):
+        return pltpu.make_async_remote_copy(
+            src_ref=link_hbm,
+            dst_ref=near_links.at[(1 + t) // 2],
+            send_sem=link_send.at[(1 + t) // 2],
+            recv_sem=link_recv.at[(1 + t) // 2],
+            device_id=(pos + t, sub),
+            device_id_type=MESH,
+        )
+
+    for t in near:
+        guarded(t, lambda t=t: link_copy(t).start())
+
     for copy in own_copies[1:]:
         copy.wait()
     for t, ds in raw_partners:
@@ -299,25 +329,30 @@
             found.append(total)
         return part, found
 
-    def outside(x, h):
+    def outside(x, h, ghost, at):
+        strip = at // SIDE
+        within = at % SIDE
         k, m = divmod(x, half)
         halves = slice(h * LANES, (h + 1) * LANES)
-        total = jnp.where(within == 0, pltpu.roll(ghosts[4, :, halves], (-x) % LANES, 1), 0.0)
+        total = jnp.where(within == 0, pltpu.roll(ghost(4, halves), (-x) % LANES, 1), 0.0)
         total = jnp.where(
-            within == SIDE - 1, pltpu.roll(ghosts[5, :, halves], SIDE - 1 - x, 1), total
+            within == SIDE - 1, pltpu.roll(ghost(5, halves), SIDE - 1 - x, 1), total
         )
         source = slice(k * LANES, (k + 1) * LANES)
         if h == 0:
-            side = pltpu.roll(ghosts[2, :, source], (-SIDE * m) % LANES, 1)
+            side = pltpu.roll(ghost(2, source), (-SIDE * m) % LANES, 1)
             total = total + jnp.where(strip == 0, side, 0.0)
         else:
-            side = pltpu.roll(ghosts[3, :, source], SIDE * (half - 1 - m), 1)
+            side = pltpu.roll(ghost(3, source), SIDE * (half - 1 - m), 1)
             total = total + jnp.where(strip == half - 1, side, 0.0)
         if x == 0:
-            total = total + ghosts[0, :, halves]
+            total = total + ghost(0, halves)
         if x == SIDE - 1:
-            total = total + ghosts[1, :, halves]
+            total = total + ghost(1, halves)
         return total
+
+    def group_ghost(d, at):
+        return ghosts[d, :, at]
 
     def value(x, h):
         return field[:, cells(x, h)]
@@ -367,22 +402,22 @@
                 first[(1 + t) * group : (2 + t) * group, spot(d, h)] = total
     gather(first)
 
-    def face_copy(window, step, t):
+    def face_copy(t):
         return pltpu.make_async_remote_copy(
             src_ref=window.at[pl.ds(group, group)],
             dst_ref=window.at[pl.ds((1 - t) * group, group)],
-            send_sem=face_send.at[step, 1 + t],
-            recv_sem=face_recv.at[step, 1 - t],
+            send_sem=face_send.at[0, 1 + t],
+            recv_sem=face_recv.at[0, 1 - t],
             device_id=(pos + t, sub),
             device_id_type=MESH,
         )
 
-    def face_landing(window, step, t):
+    def face_landing(t):
         return pltpu.make_async_remote_copy(
             src_ref=window.at[pl.ds(group, group)],
             dst_ref=window.at[pl.ds((1 + t) * group, group)],
-            send_sem=face_send.at[step, 1 + t],
-            recv_sem=face_recv.at[step, 1 + t],
+            send_sem=face_send.at[0, 1 + t],
+            recv_sem=face_recv.at[0, 1 + t],
             device_id=(pos + t, sub),
             device_id_type=MESH,
         )
@@ -407,8 +442,7 @@
             device_id_type=MESH,
         )
 
-    def send_coarse(window):
-        own = slice(group, 2 * group)
+    def send_coarse():
         left = jnp.zeros((group, LANES), jnp.float32)
         for x in range(SIDE):
             for h in range(2):
@@ -418,7 +452,7 @@
         lanes_row = lax.broadcasted_iota(jnp.int32, (8, LANES), 0)
         sums = jnp.zeros((8, LANES), jnp.float32)
         for d in range(FACES):
-            both = window[own, spot(d, 0)] + window[own, spot(d, 1)]
+            both = last_faces[0:group, spot(d, 0)] + last_faces[0:group, spot(d, 1)]
             left = left - both
             total = jnp.sum(both, axis=1, keepdims=True) / size
             line = jnp.sum(jnp.where(block, total, 0.0), axis=0, keepdims=True)
@@ -429,30 +463,87 @@
         for t in sorted(far, key=lambda t: -abs(t)):
             guarded(t, lambda t=t: coarse_copy(t).start())
 
-    windows = (window_a, window_b)
+    def part_copy(t):
+        return pltpu.make_async_remote_copy(
+            src_ref=parts_out.at[(1 + t) // 2],
+            dst_ref=parts_in.at[(1 - t) // 2],
+            send_sem=face_send.at[1, 1 + t],
+            recv_sem=face_recv.at[1, 1 - t],
+            device_id=(pos + t, sub),
+            device_id_type=MESH,
+        )
+
+    def part_landing(t):
+        return pltpu.make_async_remote_copy(
+            src_ref=parts_out.at[(1 + t) // 2],
+            dst_ref=parts_in.at[(1 + t) // 2],
+            send_sem=face_send.at[1, 1 + t],
+            recv_sem=face_recv.at[1, 1 + t],
+            device_id=(pos + t, sub),
+            device_id_type=MESH,
+        )
+
+    def own_rows(link, store):
+        for b in range(blocks):
+            for d in range(FACES):
+                place = link(b, d) - pos * group
+                place = jnp.where((place < 0) | (place >= group), group, place)
+                flipped = FLIP[d]
+                store(
+                    d * blocks + b,
+                    last_faces[pl.ds(place, 1), flipped * FACE : (flipped + 1) * FACE],
+                )
+
+    def send_part(t):
+        k = (1 + t) // 2
+
+        def store(place, value):
+            parts_out[k, place : place + 1, :] = value
+
+        own_rows(lambda b, d: near_links[k, b, d], store)
+        part_copy(t).start()
+
+    def swept(x, h):
+        here = cells(x, h)
+        fresh = base[:, here] + inv[:, here] * outside(x, h, group_ghost, group_lane)
+        field[:, here] = fresh
+        return fresh
+
     for step in range(PRE_SWEEPS):
-        window = windows[step]
-
-        def store_faces(d, h, packed):
-            window[group : 2 * group, spot(d, h)] = packed
-
-        def swept(x, h):
-            here = cells(x, h)
-            fresh = base[:, here] + inv[:, here] * outside(x, h)
-            field[:, here] = fresh
-            return fresh
-
-        pack(swept, group, group_lane, store_faces)
-        if step == PRE_SWEEPS - 1:
-            send_coarse(window)
-        for t in near:
-            guarded(t, lambda t=t: face_copy(window, step, t).start())
-        prepare()
-        if step == PRE_SWEEPS - 1:
-            break
-        for t in near:
-            guarded(t, lambda t=t: face_landing(window, step, t).wait_recv())
-        gather(window)
+        if step < PRE_SWEEPS - 1:
+
+            def store_faces(d, h, packed):
+                window[group : 2 * group, spot(d, h)] = packed
+
+            pack(swept, group, group_lane, store_faces)
+            for t in near:
+                guarded(t, lambda t=t: face_copy(t).start())
+            prepare()
+            for t in near:
+                guarded(t, lambda t=t: link_landing(t).wait_recv())
+            for t in near:
+                guarded(t, lambda t=t: face_landing(t).wait_recv())
+            gather(window)
+        else:
+
+            def store_last(d, h, packed):
+                last_faces[0:group, spot(d, h)] = packed
+
+            pack(swept, group, group_lane, store_last)
+            send_coarse()
+            for t in near:
+                guarded(t, lambda t=t: send_part(t))
+            prepare()
+
+    def store_own(place, value):
+        own_ghosts[place : place + 1, :] = value
+
+    own_rows(lambda b, d: link_ref[sub, b, d], store_own)
+    own_links = jnp.zeros((blocks, LANES), jnp.int32)
+    for b in range(blocks):
+        for d in range(FACES):
+            own_links = jnp.where((row == b) & (lane == d), link_ref[sub, b, d], own_links)
+    own_links = own_links.astype(jnp.float32)
 
     for t in far:
         guarded(t, lambda t=t: coarse_landing(t).wait_recv())
@@ -493,49 +584,57 @@
         errors = (1.0 - relaxation) * errors + driven + scaled * around
     known = turned(errors)
 
-    own_numbered = group_lane.astype(jnp.float32) + origin
-    own_error = jnp.sum(
-        jnp.where(group_lane == reach * group + group_row, known, 0.0), axis=1, keepdims=True
-    )
+    own_numbered = lane.astype(jnp.float32) + origin
+    own_at = reach * group + sub * blocks + row
+    own_error = jnp.sum(jnp.where(lane == own_at, known, 0.0), axis=1, keepdims=True)
     jumps = []
     for d in range(FACES):
-        link = message[:, d : d + 1]
+        link = own_links[:, d : d + 1]
         hit = (link == own_numbered) & (link >= 0.0)
         jumps.append(jnp.sum(jnp.where(hit, known, 0.0), axis=1, keepdims=True) - own_error)
-    plane = jnp.zeros((group, LANES), jnp.float32) + 6.0 * own_error
-    plane = plane + jnp.where(within == 0, jumps[4], 0.0)
-    plane = plane + jnp.where(within == SIDE - 1, jumps[5], 0.0)
+    own_strip = lane // SIDE
+    own_within = lane % SIDE
+    plane = jnp.zeros((blocks, LANES), jnp.float32) + 6.0 * own_error
+    plane = plane + jnp.where(own_within == 0, jumps[4], 0.0)
+    plane = plane + jnp.where(own_within == SIDE - 1, jumps[5], 0.0)
     planes = (
-        plane + jnp.where(strip == 0, jumps[2], 0.0),
-        plane + jnp.where(strip == half - 1, jumps[3], 0.0),
+        plane + jnp.where(own_strip == 0, jumps[2], 0.0),
+        plane + jnp.where(own_strip == half - 1, jumps[3], 0.0),
     )
-    kept = (1.0 - relaxation) * own_error + jnp.zeros((group, LANES), jnp.float32)
-    last = PRE_SWEEPS - 1
+    kept = (1.0 - relaxation) * own_error + jnp.zeros((blocks, LANES), jnp.float32)
+
+    def own(whole):
+        result = whole[:blocks]
+        for s in range(1, nsub):
+            result = jnp.where(sub == s, whole[s * blocks : (s + 1) * blocks], result)
+        return result
+
     for t in near:
-        guarded(t, lambda t=t: face_landing(windows[last], last, t).wait_recv())
-    gather(windows[last])
+        guarded(t, lambda t=t: part_landing(t).wait_recv())
+    own_ghosts[...] = own_ghosts[...] + parts_in[0] + parts_in[1]
+
+    def own_ghost(d, at):
+        return own_ghosts[d * blocks : (d + 1) * blocks, at]
+
     for x in range(SIDE):
         for h in range(2):
             here = cells(x, h)
-            extra = planes[h] + outside(x, h)
+            extra = planes[h] + outside(x, h, own_ghost, lane)
             if x == 0:
                 extra = extra + jumps[0]
             if x == SIDE - 1:
                 extra = extra + jumps[1]
-            whole = base[:, here] + kept + inv[:, here] * extra
-            result = whole[:blocks]
-            for s in range(1, nsub):
-                result = jnp.where(sub == s, whole[s * blocks : (s + 1) * blocks], result)
-            out_ref[:, here] = result
+            out_ref[:, here] = own(base[:, here]) + kept + own(inv[:, here]) * extra
 
     for k in range(len(inputs)):
         for ds in range(1, nsub):
             peer_copy(ds, k).wait_send()
     for t, ds in raw_partners:
         guarded(t, lambda t=t, ds=ds: raw_copy(t, ds).wait_send())
-    for step in range(PRE_SWEEPS):
-        for t in near:
-            guarded(t, lambda t=t: face_copy(windows[step], step, t).wait_send())
+    for t in near:
+        guarded(t, lambda t=t: link_copy(t).wait_send())
+        guarded(t, lambda t=t: face_copy(t).wait_send())
+        guarded(t, lambda t=t: part_copy(t).wait_send())
     for t in far:
         guarded(t, lambda t=t: coarse_copy(t).wait_send())
 
@@ -559,14 +658,18 @@
         scratch_shapes=[
             pltpu.SMEM((blocks,), jnp.int32),
             pltpu.SMEM((nsub, blocks, FACES), jnp.int32),
+            pltpu.SMEM((2, blocks, FACES), jnp.int32),
             stage,
             stage,
             stage,
             pltpu.VMEM((3 * nsub, blocks, FACES * FACE + LANES), jnp.float32),
             window,
             window,
-            window,
+            pltpu.VMEM((group + 8, FACES * FACE), jnp.float32),
+            pltpu.VMEM((2, FACES * blocks, FACE), jnp.float32),
+            pltpu.VMEM((2, FACES * blocks, FACE), jnp.float32),
             pltpu.VMEM((FACES, group, FACE), jnp.float32),
+            pltpu.VMEM((FACES * blocks, FACE), jnp.float32),
             field,
             field,
             field,
@@ -582,11 +685,18 @@
             dma((4, others)),
             dma((2 * COARSE_SWEEPS + 3,)),
             dma((2 * COARSE_SWEEPS + 3,)),
+            dma((2,)),
+            dma((2,)),
         ],
         compiler_params=pltpu.CompilerParams(
-            collective_id=0, has_side_effects=True, vmem_limit_bytes=63 * 1024 * 1024
+            collective_id=0, has_side_effects=True, vmem_limit_bytes=32 * 1024 * 1024
         ),
-    )(new_slot, face_links, pressure, source_term, coefficient)
+    )(
+        *(
+            pltpu.with_memory_space_constraint(array, pltpu.HBM)
+            for array in (new_slot, face_links, pressure, source_term, coefficient)
+        )
+    )
 
 
 def solution(mesh):

time: 21.7 us -> 19.7 us (0.908)
  Pallas kernels: 20 us -> 18.9 us
  local copies, waits for them, and re-layouts: 1.47 us -> 0.63 us
    pallas_call x1, Pallas kernels: 20 us -> 18.9 us  [on_device(): pl.pallas_call(functools.partial(kernel, count, nsub, blocks), out_shape=...]
    unnamed x1, local copies, waits for them, and re-layouts: 1.47 us -> 0.63 us
where the time goes in v4:
time: 19.7 us; the launch traced here: 19.5 us
  Pallas kernels  18.9 us (96%)
  local copies, waits for them, and re-layouts  0.63 us (3%)
    pallas_call x1, Pallas kernels, on_device(): pl.pallas_call(functools.partial(kernel, count, nsub, blocks), out_shape=...  18.9 us
    unnamed x1, local copies, waits for them, and re-layouts  0.63 us

profile of v4, /device:TPU:0, one launch (start us, length us, event | category | flops | bytes accessed | tf_op | source)
XLA Modules:
  0.0 19.5 jit_solution(8436147408097636379)
XLA Ops:
  0.0 18.9 %shard_map.55 = f32[4,4096]{1,0:T(4,128)S(1)} custom-call(s32[4]{0:T(128)} %slot_hbm.1, s32[4,6]{1,0:T(4,128)} %link_hbm.1, f32[4,4096]{1,0:T(4,128)} %p_hbm.1, f32[4,4096]{1,0:T(4,128)} %f_hbm.1, f32[4,4096]{1,0:T(4,128)} %c_hbm.1), custom_call_target="tpu_custom_call" | custom-call | tf_op jit(solution)/shard_map/pallas_call | solution.py:653
  18.9 0.6 %copy.7 = f32[4,4096]{1,0:T(4,128)} copy(f32[4,4096]{1,0:T(4,128)S(1)} %shard_map.55) | data formatting | bytes 131072

commit v5 on v4

--- a/solution.py
+++ b/solution.py
@@ -11,6 +11,7 @@
 COARSE_SWEEPS = 4
 SIDE = 16
 GREETED = 3
+UNROLL = 2
 FACE = SIDE * SIDE
 FACES = 6
 LANES = 128
@@ -193,8 +194,19 @@
     def spot(d, h):
         return slice(d * FACE + h * LANES, d * FACE + (h + 1) * LANES)
 
-    def cells(x, h):
-        return slice(x * FACE + h * LANES, x * FACE + (h + 1) * LANES)
+    def cells(x, h, shift=0):
+        return pl.ds((x + shift) * FACE + h * LANES, LANES)
+
+    def each_x(body):
+        def several(i, carried):
+            for k in range(UNROLL):
+                body(pl.multiple_of(i * (UNROLL * FACE), FACE), k)
+            return carried
+
+        lax.fori_loop(0, SIDE // UNROLL, several, 0)
+
+    def at_x(first, k, h, shift=0):
+        return pl.ds(pl.multiple_of(first + (k + shift) * FACE + h * LANES, LANES), LANES)
 
     own_slot = nsub + sub
     own_copies[0].wait()
@@ -278,16 +290,23 @@
         ]
 
     picks = chosen(0)
-    for k, target in enumerate((field, mf, mc)):
-        stage = inputs[k][1]
+    field[:, 0:FACE] = jnp.zeros((group, FACE), jnp.float32)
+    field[:, (SIDE + 1) * FACE :] = jnp.zeros((group, FACE), jnp.float32)
+    for k in range(3):
         for ds in range(1, nsub):
             peer_landing(ds, k).wait_recv()
-        for x in range(SIDE):
-            for h in range(2):
+
+    def regrid(first, k):
+        for h in range(2):
+            for stage, target, shift in ((stage_p, field, 1), (stage_f, mf, 0), (stage_c, mc, 0)):
                 total = jnp.zeros((group, LANES), jnp.float32)
                 for s, j, pick in picks:
-                    total = jnp.where(pick, stage[s, j : j + 1, cells(x, h)], total)
-                target[:, cells(x, h)] = total
+                    total = jnp.where(pick, stage[s, j : j + 1, at_x(first, k, h)], total)
+                target[:, at_x(first, k, h, shift)] = total
+                if target is mc:
+                    inv[:, at_x(first, k, h)] = relaxation / (6.0 + total)
+
+    each_x(regrid)
     for ds in range(1, nsub):
         peer_landing(ds, len(inputs) - 1).wait_recv()
 
@@ -310,24 +329,21 @@
     strip = group_lane // SIDE
     within = group_lane % SIDE
 
-    def interior(x, tile):
-        part = tile(x, 0), tile(x, 1)
+    def interior(first, k):
+        def tile(shift, h):
+            return field[:, at_x(first, k, h, 1 + shift)]
+
+        part = tile(0, 0), tile(0, 1)
         up = [pltpu.roll(v, SIDE, 1) for v in part]
         down = [pltpu.roll(v, LANES - SIDE, 1) for v in part]
-        found = []
         for h in range(2):
             total = jnp.where(within == 0, 0.0, pltpu.roll(part[h], 1, 1))
             total = total + jnp.where(within == SIDE - 1, 0.0, pltpu.roll(part[h], LANES - 1, 1))
             total = total + jnp.where(strip == 0, up[0] if h else 0.0, up[h])
-            total = total + jnp.where(
-                strip == half - 1, 0.0 if h else down[1], down[h]
-            )
-            if x > 0:
-                total = total + tile(x - 1, h)
-            if x < SIDE - 1:
-                total = total + tile(x + 1, h)
-            found.append(total)
-        return part, found
+            total = total + jnp.where(strip == half - 1, 0.0 if h else down[1], down[h])
+            total = total + tile(-1, h) + tile(1, h)
+            here = at_x(first, k, h)
+            base[:, here] = (1.0 - relaxation) * part[h] + inv[:, here] * (mf[:, here] + total)
 
     def outside(x, h, ghost, at):
         strip = at // SIDE
@@ -354,21 +370,9 @@
     def group_ghost(d, at):
         return ghosts[d, :, at]
 
-    def value(x, h):
-        return field[:, cells(x, h)]
-
     def prepare():
-        for x in range(SIDE):
-            part, found = interior(x, value)
-            for h in range(2):
-                here = cells(x, h)
-                base[:, here] = (1.0 - relaxation) * part[h] + inv[:, here] * (
-                    mf[:, here] + found[h]
-                )
-
-    for x in range(SIDE):
-        for h in range(2):
-            inv[:, cells(x, h)] = relaxation / (6.0 + mc[:, cells(x, h)])
+        each_x(interior)
+
     prepare()
 
     size = SIDE * FACE
@@ -447,7 +451,7 @@
         for x in range(SIDE):
             for h in range(2):
                 here = cells(x, h)
-                left = left + (mf[:, here] - mc[:, here] * field[:, here])
+                left = left + (mf[:, here] - mc[:, here] * field[:, cells(x, h, 1)])
         block = group_lane % group == group_row
         lanes_row = lax.broadcasted_iota(jnp.int32, (8, LANES), 0)
         sums = jnp.zeros((8, LANES), jnp.float32)
@@ -506,7 +510,7 @@
     def swept(x, h):
         here = cells(x, h)
         fresh = base[:, here] + inv[:, here] * outside(x, h, group_ghost, group_lane)
-        field[:, here] = fresh
+        field[:, cells(x, h, 1)] = fresh
         return fresh
 
     for step in range(PRE_SWEEPS):
@@ -647,6 +651,7 @@
     others = max(1, nsub - 1)
     stage = pltpu.VMEM((nsub, blocks, size), jnp.float32)
     field = pltpu.VMEM((group, size), jnp.float32)
+    padded = pltpu.VMEM((group, size + 2 * FACE), jnp.float32)
     window = pltpu.VMEM((3 * group + 8, FACES * FACE), jnp.float32)
     dma = pltpu.SemaphoreType.DMA
     hbm = pl.BlockSpec(memory_space=pltpu.HBM)
@@ -673,7 +678,7 @@
             field,
             field,
             field,
-            field,
+            padded,
             field,
             pltpu.VMEM((2 * COARSE_SWEEPS + 3, group + 8, LANES), jnp.float32),
             dma((5,)),

time: 19.7 us -> 19.3 us (0.980)
  Pallas kernels: 18.9 us -> 18.5 us
    pallas_call x1, Pallas kernels: 18.9 us -> 18.5 us  [on_device(): pl.pallas_call(functools.partial(kernel, count, nsub, blocks), out_shape=...]
where the time goes in v5:
time: 19.3 us; the launch traced here: 19.1 us
  Pallas kernels  18.5 us (96%)
  local copies, waits for them, and re-layouts  0.63 us (3%)
    pallas_call x1, Pallas kernels, on_device(): pl.pallas_call(functools.partial(kernel, count, nsub, blocks), out_shape=...  18.5 us
    unnamed x1, local copies, waits for them, and re-layouts  0.63 us

profile of v5, /device:TPU:0, one launch (start us, length us, event | category | flops | bytes accessed | tf_op | source)
XLA Modules:
  0.0 19.1 jit_solution(18068594362135887929)
XLA Ops:
  0.0 18.5 %shard_map.55 = f32[4,4096]{1,0:T(4,128)S(1)} custom-call(s32[4]{0:T(128)} %slot_hbm.1, s32[4,6]{1,0:T(4,128)} %link_hbm.1, f32[4,4096]{1,0:T(4,128)} %p_hbm.1, f32[4,4096]{1,0:T(4,128)} %f_hbm.1, f32[4,4096]{1,0:T(4,128)} %c_hbm.1), custom_call_target="tpu_custom_call" | custom-call | tf_op jit(solution)/shard_map/pallas_call | solution.py:658
  18.5 0.6 %copy.7 = f32[4,4096]{1,0:T(4,128)} copy(f32[4,4096]{1,0:T(4,128)S(1)} %shard_map.55) | data formatting | bytes 131072

commit v6 on v5

--- a/solution.py
+++ b/solution.py
@@ -81,23 +81,6 @@
         else:
             pl.when(exists(t))(action)
 
-    barrier = pltpu.get_barrier_semaphore()
-    expected = 0
-    for t in sorted(range(-greeted, greeted + 1), key=abs):
-        for ds in range(nsub if abs(t) <= 1 else 1):
-            if t or ds:
-
-                def greet(t=t, ds=ds):
-                    pl.semaphore_signal(
-                        barrier,
-                        inc=1,
-                        device_id=(pos + t, lax.rem(sub + ds, nsub)),
-                        device_id_type=MESH,
-                    )
-
-                guarded(t, greet)
-                expected = expected + (exists(t).astype(jnp.int32) if t else 1)
-
     inputs = (
         (p_hbm, stage_p),
         (f_hbm, stage_f),
@@ -110,6 +93,24 @@
     ]
     own_slots = pltpu.make_async_copy(slot_hbm, slot_ref, local_sem.at[len(inputs)])
     own_copies[0].start()
+
+    barrier = pltpu.get_barrier_semaphore()
+    expected = 0
+    for t in sorted(range(-greeted, greeted + 1), key=abs):
+        for ds in range(nsub if abs(t) <= 1 else 1):
+            if t or ds:
+
+                def greet(t=t, ds=ds):
+                    pl.semaphore_signal(
+                        barrier,
+                        inc=1,
+                        device_id=(pos + t, lax.rem(sub + ds, nsub)),
+                        device_id_type=MESH,
+                    )
+
+                guarded(t, greet)
+                expected = expected + (exists(t).astype(jnp.int32) if t else 1)
+
     own_slots.start()
     for copy in own_copies[1:]:
         copy.start()
@@ -244,14 +245,6 @@
             device_id_type=MESH,
         )
 
-    raw_partners = [(t, ds) for t in (-1, 1, 0) for ds in range(nsub) if t or ds]
-    pl.semaphore_wait(barrier, expected)
-    for t, ds in raw_partners:
-        guarded(t, lambda t=t, ds=ds: raw_copy(t, ds).start())
-    for k in range(len(inputs)):
-        for ds in range(1, nsub):
-            peer_copy(ds, k).start()
-
     def link_copy(t):
         return pltpu.make_async_remote_copy(
             src_ref=link_hbm,
@@ -272,8 +265,21 @@
             device_id_type=MESH,
         )
 
+    raw_partners = [(t, ds) for t in (-1, 1, 0) for ds in range(nsub) if t or ds]
+    pl.semaphore_wait(barrier, expected)
     for t in near:
-        guarded(t, lambda t=t: link_copy(t).start())
+
+        @pl.when(exists(t))
+        def _(t=t):
+            for ds in range(nsub):
+                raw_copy(t, ds).start()
+            link_copy(t).start()
+
+    for ds in range(1, nsub):
+        raw_copy(0, ds).start()
+    for k in range(len(inputs)):
+        for ds in range(1, nsub):
+            peer_copy(ds, k).start()
 
     for copy in own_copies[1:]:
         copy.wait()
@@ -393,8 +399,12 @@
 
     for t in (0, -1, 1):
         if t:
-            for ds in range(nsub):
-                guarded(t, lambda t=t, ds=ds: raw_landing(t, ds).wait_recv())
+
+            @pl.when(exists(t))
+            def _(t=t):
+                for ds in range(nsub):
+                    raw_landing(t, ds).wait_recv()
+
         picks = chosen(t)
         for d in range(FACES):
             for h in range(2):
@@ -524,9 +534,12 @@
                 guarded(t, lambda t=t: face_copy(t).start())
             prepare()
             for t in near:
-                guarded(t, lambda t=t: link_landing(t).wait_recv())
-            for t in near:
-                guarded(t, lambda t=t: face_landing(t).wait_recv())
+
+                @pl.when(exists(t))
+                def _(t=t):
+                    link_landing(t).wait_recv()
+                    face_landing(t).wait_recv()
+
             gather(window)
         else:
 
@@ -552,10 +565,11 @@
     for t in far:
         guarded(t, lambda t=t: coarse_landing(t).wait_recv())
 
-    shown = coarse[:, 0:group, :]
-    shape = (2 * reach + 1, group, LANES)
+    count_near = 2 * reach - 1
+    shown = coarse[1 : 1 + count_near, 0:group, :]
+    shape = (count_near, group, LANES)
     column = lax.broadcasted_iota(jnp.int32, shape, 2)
-    index = lax.broadcasted_iota(jnp.int32, shape, 0) * group + lax.broadcasted_iota(
+    index = (lax.broadcasted_iota(jnp.int32, shape, 0) + 1) * group + lax.broadcasted_iota(
         jnp.int32, shape, 1
     )
     origin = ((pos - reach) * group).astype(jnp.float32)
@@ -576,17 +590,39 @@
     diags = shown[:, :, FACES + 1 : FACES + 2]
     diags = jnp.where(diags > 0.0, diags, 1.0)
 
-    def turned(values):
-        spread = jnp.where(index == column, values, 0.0)
+    def own(whole):
+        result = whole[:blocks]
+        for s in range(1, nsub):
+            result = jnp.where(sub == s, whole[s * blocks : (s + 1) * blocks], result)
+        return result
+
+    for t in near:
+        guarded(t, lambda t=t: part_landing(t).wait_recv())
+    own_ghosts[...] = own_ghosts[...] + parts_in[0] + parts_in[1]
+
+    def own_ghost(d, at):
+        return own_ghosts[d * blocks : (d + 1) * blocks, at]
+
+    for x in range(SIDE):
+        for h in range(2):
+            here = cells(x, h)
+            out_ref[:, here] = own(base[:, here]) + own(inv[:, here]) * outside(
+                x, h, own_ghost, lane
+            )
+
+    def turned(values, edge):
+        kept = slice(edge, count_near - edge)
+        spread = jnp.where(index[kept] == column[kept], values, 0.0)
         return jnp.sum(jnp.sum(spread, axis=0), axis=0, keepdims=True)
 
     scaled = relaxation / diags
     driven = scaled * residuals
     errors = driven
     for step in range(1, COARSE_SWEEPS):
-        around = jnp.sum(linked * turned(errors)[None], axis=2, keepdims=True)
-        errors = (1.0 - relaxation) * errors + driven + scaled * around
-    known = turned(errors)
+        kept = slice(step, count_near - step)
+        around = jnp.sum(linked[kept] * turned(errors, step - 1)[None], axis=2, keepdims=True)
+        errors = (1.0 - relaxation) * errors[1:-1] + driven[kept] + scaled[kept] * around
+    known = turned(errors, COARSE_SWEEPS - 1)
 
     own_numbered = lane.astype(jnp.float32) + origin
     own_at = reach * group + sub * blocks + row
@@ -607,28 +643,15 @@
     )
     kept = (1.0 - relaxation) * own_error + jnp.zeros((blocks, LANES), jnp.float32)
 
-    def own(whole):
-        result = whole[:blocks]
-        for s in range(1, nsub):
-            result = jnp.where(sub == s, whole[s * blocks : (s + 1) * blocks], result)
-        return result
-
-    for t in near:
-        guarded(t, lambda t=t: part_landing(t).wait_recv())
-    own_ghosts[...] = own_ghosts[...] + parts_in[0] + parts_in[1]
-
-    def own_ghost(d, at):
-        return own_ghosts[d * blocks : (d + 1) * blocks, at]
-
     for x in range(SIDE):
         for h in range(2):
             here = cells(x, h)
-            extra = planes[h] + outside(x, h, own_ghost, lane)
+            extra = planes[h]
             if x == 0:
                 extra = extra + jumps[0]
             if x == SIDE - 1:
                 extra = extra + jumps[1]
-            out_ref[:, here] = own(base[:, here]) + kept + own(inv[:, here]) * extra
+            out_ref[:, here] = out_ref[:, here] + (kept + own(inv[:, here]) * extra)
 
     for k in range(len(inputs)):
         for ds in range(1, nsub):

time: 19.3 us -> 19 us (0.984)
  Pallas kernels: 18.5 us -> 18.2 us
    pallas_call x1, Pallas kernels: 18.5 us -> 18.2 us  [on_device(): pl.pallas_call(functools.partial(kernel, count, nsub, blocks), out_shape=...]
where the time goes in v6:
time: 19 us; the launch traced here: 18.9 us
  Pallas kernels  18.2 us (96%)
  local copies, waits for them, and re-layouts  0.63 us (3%)
    pallas_call x1, Pallas kernels, on_device(): pl.pallas_call(functools.partial(kernel, count, nsub, blocks), out_shape=...  18.2 us
    unnamed x1, local copies, waits for them, and re-layouts  0.63 us

profile of v6, /device:TPU:0, one launch (start us, length us, event | category | flops | bytes accessed | tf_op | source)
XLA Modules:
  0.0 18.9 jit_solution(13727092205203942065)
XLA Ops:
  0.0 18.2 %shard_map.55 = f32[4,4096]{1,0:T(4,128)S(1)} custom-call(s32[4]{0:T(128)} %slot_hbm.1, s32[4,6]{1,0:T(4,128)} %link_hbm.1, f32[4,4096]{1,0:T(4,128)} %p_hbm.1, f32[4,4096]{1,0:T(4,128)} %f_hbm.1, f32[4,4096]{1,0:T(4,128)} %c_hbm.1), custom_call_target="tpu_custom_call" | custom-call | tf_op jit(solution)/shard_map/pallas_call | solution.py:681
  18.3 0.6 %copy.7 = f32[4,4096]{1,0:T(4,128)} copy(f32[4,4096]{1,0:T(4,128)S(1)} %shard_map.55) | data formatting | bytes 131072

commit v7 on v6

--- a/solution.py
+++ b/solution.py
@@ -533,10 +533,17 @@
             for t in near:
                 guarded(t, lambda t=t: face_copy(t).start())
             prepare()
+            for ds in range(1, nsub):
+                for k in range(len(inputs)):
+                    peer_copy(ds, k).wait_send()
+                raw_copy(0, ds).wait_send()
             for t in near:
 
                 @pl.when(exists(t))
                 def _(t=t):
+                    for ds in range(nsub):
+                        raw_copy(t, ds).wait_send()
+                    link_copy(t).wait_send()
                     link_landing(t).wait_recv()
                     face_landing(t).wait_recv()
 
@@ -562,8 +569,15 @@
             own_links = jnp.where((row == b) & (lane == d), link_ref[sub, b, d], own_links)
     own_links = own_links.astype(jnp.float32)
 
+    for t in near:
+        guarded(t, lambda t=t: face_copy(t).wait_send())
     for t in far:
-        guarded(t, lambda t=t: coarse_landing(t).wait_recv())
+
+        @pl.when(exists(t))
+        def _(t=t):
+            coarse_copy(t).wait_send()
+            coarse_landing(t).wait_recv()
+
 
     count_near = 2 * reach - 1
     shown = coarse[1 : 1 + count_near, 0:group, :]
@@ -597,7 +611,12 @@
         return result
 
     for t in near:
-        guarded(t, lambda t=t: part_landing(t).wait_recv())
+
+        @pl.when(exists(t))
+        def _(t=t):
+            part_copy(t).wait_send()
+            part_landing(t).wait_recv()
+
     own_ghosts[...] = own_ghosts[...] + parts_in[0] + parts_in[1]
 
     def own_ghost(d, at):
@@ -652,18 +671,6 @@
             if x == SIDE - 1:
                 extra = extra + jumps[1]
             out_ref[:, here] = out_ref[:, here] + (kept + own(inv[:, here]) * extra)
-
-    for k in range(len(inputs)):
-        for ds in range(1, nsub):
-            peer_copy(ds, k).wait_send()
-    for t, ds in raw_partners:
-        guarded(t, lambda t=t, ds=ds: raw_copy(t, ds).wait_send())
-    for t in near:
-        guarded(t, lambda t=t: link_copy(t).wait_send())
-        guarded(t, lambda t=t: face_copy(t).wait_send())
-        guarded(t, lambda t=t: part_copy(t).wait_send())
-    for t in far:
-        guarded(t, lambda t=t: coarse_copy(t).wait_send())
 
 
 def on_device(pressure, source_term, coefficient, new_slot, face_links):

time: 19 us -> 19 us (level)
  no operation moved by 1% of the time
where the time goes in v7:
time: 19 us; the launch traced here: 18.8 us
  Pallas kernels  18.2 us (96%)
  local copies, waits for them, and re-layouts  0.63 us (3%)
    pallas_call x1, Pallas kernels, on_device(): pl.pallas_call(functools.partial(kernel, count, nsub, blocks), out_shape=...  18.2 us
    unnamed x1, local copies, waits for them, and re-layouts  0.63 us

profile of v7, /device:TPU:0, one launch (start us, length us, event | category | flops | bytes accessed | tf_op | source)
XLA Modules:
  0.0 18.8 jit_solution(12871554742805803710)
XLA Ops:
  0.0 18.2 %shard_map.55 = f32[4,4096]{1,0:T(4,128)S(1)} custom-call(s32[4]{0:T(128)} %slot_hbm.1, s32[4,6]{1,0:T(4,128)} %link_hbm.1, f32[4,4096]{1,0:T(4,128)} %p_hbm.1, f32[4,4096]{1,0:T(4,128)} %f_hbm.1, f32[4,4096]{1,0:T(4,128)} %c_hbm.1), custom_call_target="tpu_custom_call" | custom-call | tf_op jit(solution)/shard_map/pallas_call | solution.py:688
  18.2 0.6 %copy.7 = f32[4,4096]{1,0:T(4,128)} copy(f32[4,4096]{1,0:T(4,128)S(1)} %shard_map.55) | data formatting | bytes 131072

commit v8 on v7

--- a/solution.py
+++ b/solution.py
@@ -39,7 +39,8 @@
     stage_c,
     raw,
     first,
-    window,
+    window_low,
+    window_high,
     last_faces,
     parts_out,
     parts_in,
@@ -69,6 +70,7 @@
     reach = COARSE_SWEEPS + 1
     greeted = GREETED
     wall = 3 * group
+    windows = (window_low, window_high)
     near = (-1, 1)
     far = [t for t in range(-reach, reach + 1) if t]
 
@@ -119,13 +121,15 @@
         window[rows] = jnp.zeros((rows.stop - rows.start,) + window.shape[1:], jnp.float32)
 
     clear(first, slice(wall, wall + 8))
-    clear(window, slice(wall, wall + 8))
+    for window in windows:
+        clear(window, slice(wall, wall + 8))
     clear(last_faces, slice(group, group + 8))
     for t in near:
 
         @pl.when(jnp.logical_not(exists(t)))
         def _(t=t):
-            clear(window, slice((t + 1) * group, (t + 2) * group))
+            for window in windows:
+                clear(window, slice((t + 1) * group, (t + 2) * group))
             clear(parts_in, slice((t + 1) // 2, (t + 1) // 2 + 1))
             clear(raw, slice((t + 1) * nsub, (t + 2) * nsub))
 
@@ -164,33 +168,35 @@
     group_row = lax.broadcasted_iota(jnp.int32, (group, LANES), 0)
     half = SIDE // 2
 
-    def pack(tile, rows, at, store):
+    def pack_half(h, tile, rows, at, store):
         strip = at // SIDE
         within = at % SIDE
         zero = jnp.zeros((rows, LANES), jnp.float32)
-        y_low = [zero, zero]
-        y_high = [zero, zero]
-        z_low = [zero, zero]
-        z_high = [zero, zero]
+        z_low = z_high = zero
+        y_side = [zero, zero]
         for x in range(SIDE):
-            part = tile(x, 0), tile(x, 1)
+            part = tile(x, h)
             k, m = divmod(x, half)
-            for h in range(2):
-                if x == 0:
-                    store(0, h, part[h])
-                if x == SIDE - 1:
-                    store(1, h, part[h])
-                z_low[h] = jnp.where(within == x, pltpu.roll(part[h], x, 1), z_low[h])
-                z_high[h] = jnp.where(
-                    within == x, pltpu.roll(part[h], (x - SIDE + 1) % LANES, 1), z_high[h]
-                )
-            y_low[k] = jnp.where(strip == m, pltpu.roll(part[0], SIDE * m, 1), y_low[k])
-            y_high[k] = jnp.where(
-                strip == m, pltpu.roll(part[1], (SIDE * (m + 1)) % LANES, 1), y_high[k]
-            )
-        for d, packed in ((2, y_low), (3, y_high), (4, z_low), (5, z_high)):
-            for h in range(2):
-                store(d, h, packed[h])
+            if x == 0:
+                store(0, h, part)
+            if x == SIDE - 1:
+                store(1, h, part)
+            z_low = jnp.where(within == x, pltpu.roll(part, x, 1), z_low)
+            z_high = jnp.where(within == x, pltpu.roll(part, (x - SIDE + 1) % LANES, 1), z_high)
+            shift = SIDE * (m + h) % LANES
+            y_side[k] = jnp.where(strip == m, pltpu.roll(part, shift, 1), y_side[k])
+        store(4, h, z_low)
+        store(5, h, z_high)
+        for k in range(2):
+            store(2 + h, k, y_side[k])
+
+    def pack(tile, rows, at, store):
+        for h in range(2):
+            pack_half(h, tile, rows, at, store)
+
+    def half_spot(d, h):
+        tile = {0: 0, 1: 1, 4: 2, 5: 3}[d] if d not in (2, 3) else 4 + h
+        return slice(tile * LANES, (tile + 1) * LANES)
 
     def spot(d, h):
         return slice(d * FACE + h * LANES, d * FACE + (h + 1) * LANES)
@@ -331,6 +337,17 @@
             ghosts[d, pl.ds(b, 1), :] = window[
                 pl.ds(place, 1), flipped * FACE : (flipped + 1) * FACE
             ]
+
+    def gather_half(h):
+        for b, d, place in places:
+            flipped = FLIP[d]
+            if flipped in (2, 3):
+                if flipped == 2 + h:
+                    ghosts[d, pl.ds(b, 1), :] = windows[h][pl.ds(place, 1), 4 * LANES : 6 * LANES]
+            else:
+                first_lane = half_spot(flipped, h).start
+                pair = windows[h][pl.ds(place, 1), first_lane : first_lane + FACE]
+                ghosts[d, pl.ds(b, 1), h * LANES : (h + 1) * LANES] = pair[:, :LANES]
 
     strip = group_lane // SIDE
     within = group_lane % SIDE
@@ -416,22 +433,22 @@
                 first[(1 + t) * group : (2 + t) * group, spot(d, h)] = total
     gather(first)
 
-    def face_copy(t):
-        return pltpu.make_async_remote_copy(
-            src_ref=window.at[pl.ds(group, group)],
-            dst_ref=window.at[pl.ds((1 - t) * group, group)],
-            send_sem=face_send.at[0, 1 + t],
-            recv_sem=face_recv.at[0, 1 - t],
+    def face_copy(t, h):
+        return pltpu.make_async_remote_copy(
+            src_ref=windows[h].at[pl.ds(group, group)],
+            dst_ref=windows[h].at[pl.ds((1 - t) * group, group)],
+            send_sem=face_send.at[h, 1 + t],
+            recv_sem=face_recv.at[h, 1 - t],
             device_id=(pos + t, sub),
             device_id_type=MESH,
         )
 
-    def face_landing(t):
-        return pltpu.make_async_remote_copy(
-            src_ref=window.at[pl.ds(group, group)],
-            dst_ref=window.at[pl.ds((1 + t) * group, group)],
-            send_sem=face_send.at[0, 1 + t],
-            recv_sem=face_recv.at[0, 1 + t],
+    def face_landing(t, h):
+        return pltpu.make_async_remote_copy(
+            src_ref=windows[h].at[pl.ds(group, group)],
+            dst_ref=windows[h].at[pl.ds((1 + t) * group, group)],
+            send_sem=face_send.at[h, 1 + t],
+            recv_sem=face_recv.at[h, 1 + t],
             device_id=(pos + t, sub),
             device_id_type=MESH,
         )
@@ -481,8 +498,8 @@
         return pltpu.make_async_remote_copy(
             src_ref=parts_out.at[(1 + t) // 2],
             dst_ref=parts_in.at[(1 - t) // 2],
-            send_sem=face_send.at[1, 1 + t],
-            recv_sem=face_recv.at[1, 1 - t],
+            send_sem=face_send.at[2, 1 + t],
+            recv_sem=face_recv.at[2, 1 - t],
             device_id=(pos + t, sub),
             device_id_type=MESH,
         )
@@ -491,8 +508,8 @@
         return pltpu.make_async_remote_copy(
             src_ref=parts_out.at[(1 + t) // 2],
             dst_ref=parts_in.at[(1 + t) // 2],
-            send_sem=face_send.at[1, 1 + t],
-            recv_sem=face_recv.at[1, 1 + t],
+            send_sem=face_send.at[2, 1 + t],
+            recv_sem=face_recv.at[2, 1 + t],
             device_id=(pos + t, sub),
             device_id_type=MESH,
         )
@@ -526,12 +543,14 @@
     for step in range(PRE_SWEEPS):
         if step < PRE_SWEEPS - 1:
 
-            def store_faces(d, h, packed):
-                window[group : 2 * group, spot(d, h)] = packed
-
-            pack(swept, group, group_lane, store_faces)
-            for t in near:
-                guarded(t, lambda t=t: face_copy(t).start())
+            for side in range(2):
+
+                def store_faces(d, h, packed):
+                    windows[side][group : 2 * group, half_spot(d, h)] = packed
+
+                pack_half(side, swept, group, group_lane, store_faces)
+                for t in near:
+                    guarded(t, lambda t=t: face_copy(t, side).start())
             prepare()
             for ds in range(1, nsub):
                 for k in range(len(inputs)):
@@ -545,9 +564,12 @@
                         raw_copy(t, ds).wait_send()
                     link_copy(t).wait_send()
                     link_landing(t).wait_recv()
-                    face_landing(t).wait_recv()
-
-            gather(window)
+                    face_landing(t, 0).wait_recv()
+
+            gather_half(0)
+            for t in near:
+                guarded(t, lambda t=t: face_landing(t, 1).wait_recv())
+            gather_half(1)
         else:
 
             def store_last(d, h, packed):
@@ -570,7 +592,8 @@
     own_links = own_links.astype(jnp.float32)
 
     for t in near:
-        guarded(t, lambda t=t: face_copy(t).wait_send())
+        for side in range(2):
+            guarded(t, lambda t=t, side=side: face_copy(t, side).wait_send())
     for t in far:
 
         @pl.when(exists(t))
@@ -683,6 +706,7 @@
     field = pltpu.VMEM((group, size), jnp.float32)
     padded = pltpu.VMEM((group, size + 2 * FACE), jnp.float32)
     window = pltpu.VMEM((3 * group + 8, FACES * FACE), jnp.float32)
+    half_window = pltpu.VMEM((3 * group + 8, FACES * LANES), jnp.float32)
     dma = pltpu.SemaphoreType.DMA
     hbm = pl.BlockSpec(memory_space=pltpu.HBM)
     return pl.pallas_call(
@@ -699,7 +723,8 @@
             stage,
             pltpu.VMEM((3 * nsub, blocks, FACES * FACE + LANES), jnp.float32),
             window,
-            window,
+            half_window,
+            half_window,
             pltpu.VMEM((group + 8, FACES * FACE), jnp.float32),
             pltpu.VMEM((2, FACES * blocks, FACE), jnp.float32),
             pltpu.VMEM((2, FACES * blocks, FACE), jnp.float32),
@@ -714,8 +739,8 @@
             dma((5,)),
             dma((3 * nsub,)),
             dma((3 * nsub,)),
-            dma((PRE_SWEEPS, 3)),
-            dma((PRE_SWEEPS, 3)),
+            dma((3, 3)),
+            dma((3, 3)),
             dma((4, others)),
             dma((4, others)),
             dma((2 * COARSE_SWEEPS + 3,)),

time: 19 us -> 19.2 us (1.011)
  Pallas kernels: 18.2 us -> 18.4 us
    pallas_call x1, Pallas kernels: 18.2 us -> 18.4 us  [on_device(): pl.pallas_call(functools.partial(kernel, count, nsub, blocks), out_shape=...]
where the time goes in v8:
time: 19.2 us; the launch traced here: 19.1 us
  Pallas kernels  18.4 us (96%)
  local copies, waits for them, and re-layouts  0.63 us (3%)
    pallas_call x1, Pallas kernels, on_device(): pl.pallas_call(functools.partial(kernel, count, nsub, blocks), out_shape=...  18.4 us
    unnamed x1, local copies, waits for them, and re-layouts  0.63 us

profile of v8, /device:TPU:0, one launch (start us, length us, event | category | flops | bytes accessed | tf_op | source)
XLA Modules:
  0.0 19.1 jit_solution(3966637714953215544)
XLA Ops:
  0.0 18.4 %shard_map.55 = f32[4,4096]{1,0:T(4,128)S(1)} custom-call(s32[4]{0:T(128)} %slot_hbm.1, s32[4,6]{1,0:T(4,128)} %link_hbm.1, f32[4,4096]{1,0:T(4,128)} %p_hbm.1, f32[4,4096]{1,0:T(4,128)} %f_hbm.1, f32[4,4096]{1,0:T(4,128)} %c_hbm.1), custom_call_target="tpu_custom_call" | custom-call | tf_op jit(solution)/shard_map/pallas_call | solution.py:712
  18.4 0.6 %copy.7 = f32[4,4096]{1,0:T(4,128)} copy(f32[4,4096]{1,0:T(4,128)S(1)} %shard_map.55) | data formatting | bytes 131072

commit v9 on v7

--- a/solution.py
+++ b/solution.py
@@ -11,7 +11,7 @@
 COARSE_SWEEPS = 4
 SIDE = 16
 GREETED = 3
-UNROLL = 2
+UNROLL = 4
 FACE = SIDE * SIDE
 FACES = 6
 LANES = 128

time: 19 us -> 19 us (level)
  no operation moved by 1% of the time
where the time goes in v9:
time: 19 us; the launch traced here: 18.8 us
  Pallas kernels  18.2 us (96%)
  local copies, waits for them, and re-layouts  0.63 us (3%)
    pallas_call x1, Pallas kernels, on_device(): pl.pallas_call(functools.partial(kernel, count, nsub, blocks), out_shape=...  18.2 us
    unnamed x1, local copies, waits for them, and re-layouts  0.63 us

profile of v9, /device:TPU:0, one launch (start us, length us, event | category | flops | bytes accessed | tf_op | source)
XLA Modules:
  0.0 18.8 jit_solution(4133987444785371644)
XLA Ops:
  0.0 18.2 %shard_map.55 = f32[4,4096]{1,0:T(4,128)S(1)} custom-call(s32[4]{0:T(128)} %slot_hbm.1, s32[4,6]{1,0:T(4,128)} %link_hbm.1, f32[4,4096]{1,0:T(4,128)} %p_hbm.1, f32[4,4096]{1,0:T(4,128)} %f_hbm.1, f32[4,4096]{1,0:T(4,128)} %c_hbm.1), custom_call_target="tpu_custom_call" | custom-call | tf_op jit(solution)/shard_map/pallas_call | solution.py:688
  18.2 0.6 %copy.7 = f32[4,4096]{1,0:T(4,128)} copy(f32[4,4096]{1,0:T(4,128)S(1)} %shard_map.55) | data formatting | bytes 131072

commit v10 on v9

--- a/solution.py
+++ b/solution.py
@@ -11,7 +11,7 @@
 COARSE_SWEEPS = 4
 SIDE = 16
 GREETED = 3
-UNROLL = 4
+UNROLL = 8
 FACE = SIDE * SIDE
 FACES = 6
 LANES = 128

time: 19 us -> 19 us (level)
  no operation moved by 1% of the time
where the time goes in v10:
time: 19 us; the launch traced here: 18.8 us
  Pallas kernels  18.2 us (96%)
  local copies, waits for them, and re-layouts  0.63 us (3%)
    pallas_call x1, Pallas kernels, on_device(): pl.pallas_call(functools.partial(kernel, count, nsub, blocks), out_shape=...  18.2 us
    unnamed x1, local copies, waits for them, and re-layouts  0.63 us

profile of v10, /device:TPU:0, one launch (start us, length us, event | category | flops | bytes accessed | tf_op | source)
XLA Modules:
  0.0 18.8 jit_solution(13306546140186103433)
XLA Ops:
  0.0 18.2 %shard_map.55 = f32[4,4096]{1,0:T(4,128)S(1)} custom-call(s32[4]{0:T(128)} %slot_hbm.1, s32[4,6]{1,0:T(4,128)} %link_hbm.1, f32[4,4096]{1,0:T(4,128)} %p_hbm.1, f32[4,4096]{1,0:T(4,128)} %f_hbm.1, f32[4,4096]{1,0:T(4,128)} %c_hbm.1), custom_call_target="tpu_custom_call" | custom-call | tf_op jit(solution)/shard_map/pallas_call | solution.py:688
  18.2 0.6 %copy.7 = f32[4,4096]{1,0:T(4,128)} copy(f32[4,4096]{1,0:T(4,128)S(1)} %shard_map.55) | data formatting | bytes 131072
